TPU v7x, 128 devices: a whole 4x4x4 slice. The times are simulated.
128 devices in a mesh: mem: 4 (over y_lo, core), tile: 32 (over x, z, y_hi).
Axes of the slice: x: 4, y: 4 (y_hi: 2, y_lo: 2; y = y_hi * 2 + y_lo), z: 4, core: 2. Of those that a mesh axis runs over, the one named last changes fastest.
Arguments:
- member_collection: bfloat16 [256, 8, 256, 128], P('mem', None, 'tile'), may hold values from -6 to 6
- spreading_ratio: float32 [8, 256, 128], P(None, 'tile'), may hold values from 0.005 to 0.07
- transport_ratio_row: float32 [8], replicated, may hold values from 0.1 to 0.35
- transport_ratio_column: float32 [8], replicated, may hold values from 0.1 to 0.35
- obs_patch: int32 [32768], P(('mem', 'tile')), may hold values from 0 to 512, as said below
Outputs:
- forecast: bfloat16 [256, 8, 256, 128], P('mem', None, 'tile')
Inputs may be any that keep to these rules, and one draw needn't show every extreme that they name: `obs_patch`: a value of 512 marks an empty slot that no patch counts.
All inputs are finite; a program needn't handle non-finite values.
Results may differ from a plain program's by a relative error of at most 0.001.
The roundings to bfloat16 on the way count: a program that leaves them out, or rounds other values in their place, can miss the bound.
Values may be sent and summed in bfloat16 or wider, within the bound.
A program may use at most 64 MiB of HBM per device.

v0:
```python
import jax
import jax.numpy as jnp
from jax import lax
from jax.experimental import pallas as pl
from jax.experimental.pallas import tpu as pltpu
from jax.sharding import PartitionSpec as P

F32 = jnp.float32
BF16 = jnp.bfloat16
MESH = pl.DeviceIdType.MESH
VMEM_LIMIT = 50 * 1024 * 1024
NS_ITERS = 14
PLAIN_NORM = 2500.0
CONVERGED = 1e-6
NT = (((1,), (1,)), ((), ()))
TN = (((0,), (0,)), ((), ()))


def place():
    tile = lax.axis_index("tile")
    mem = lax.axis_index("mem")
    ring = tile // 2
    half = lax.rem(tile, 2)
    return ring, half, mem, half * 4 + mem


def target(ring, slot):
    return {"mem": lax.rem(slot, 4), "tile": 2 * ring + slot // 4}


def remote(src, dst, send_sem, recv_sem, ring, slot):
    return pltpu.make_async_remote_copy(
        src_ref=src,
        dst_ref=dst,
        send_sem=send_sem,
        recv_sem=recv_sem,
        device_id=target(ring, slot),
        device_id_type=MESH,
    )


def signal(sem, ring, slot):
    pl.semaphore_signal(sem, inc=1, device_id=target(ring, slot), device_id_type=MESH)


def stencil(c, bx, ax, by, ay, s, sx, sy):
    return c - sx * (c - bx) - sy * (c - by) + s * (ax + bx + ay + by - 4.0 * c)


def rounded(x):
    return x.astype(BF16).astype(F32)


def loop(lower, upper, body):
    def step(i, carry):
        body(i)
        return carry

    lax.fori_loop(lower, upper, step, 0)


def forecast_kernel(
    rings,
    v_ref,
    spread_ref,
    sx_ref,
    sy_ref,
    obs_ref,
    anom_ref,
    cen_ref,
    avg_ref,
    wt_ref,
    coef_ref,
    snd,
    rcv,
    u0,
    u1,
    coef,
    spr,
    cst,
    cra,
    crb,
    gpk,
    gab,
    gbe,
    gle,
    gri,
    main_send,
    main_recv,
    halo_send,
    halo_recv,
    spr_send,
    spr_recv,
    cnt_send,
    cnt_recv,
    sum_send,
    sum_recv,
    gram_send,
    gram_recv,
):
    ring, half, mem, slot = place()
    above = lax.rem(ring + rings - 1, rings)
    below = lax.rem(ring + 1, rings)
    beside = lax.rem(ring + rings + 2 * half - 1, rings)

    barrier = pltpu.get_barrier_semaphore()
    loop(1, 8, lambda j: signal(barrier, ring, lax.rem(slot + j, 8)))
    loop(1, rings, lambda j: signal(barrier, lax.rem(ring + j, rings), slot))
    loop(0, 4, lambda j: signal(barrier, above, 4 + j))
    loop(0, 4, lambda j: signal(barrier, below, j))

    obs = obs_ref[...]
    in_ring = lax.broadcasted_iota(jnp.int32, (rings, 256), 0) == obs // 32
    in_patch = lax.broadcasted_iota(jnp.int32, (128, 256), 0) == lax.rem(obs, 32)
    tally = lax.dot_general(
        in_ring.astype(F32).astype(BF16), in_patch.astype(F32).astype(BF16), NT,
        preferred_element_type=F32,
    )
    for r in range(rings):
        cst[r] = jnp.broadcast_to(tally[r : r + 1, :], (8, 128))
    cra[ring] = cst[ring]
    spr[pl.ds(8 + 8 * half, 8)] = spread_ref[...]

    pl.semaphore_wait(barrier, 7 + rings - 1 + 8)

    spr_here = remote(
        spread_ref, spr.at[pl.ds(8 + 8 * half, 8)], spr_send.at[0], spr_recv.at[0],
        ring, (1 - half) * 4 + mem,
    )
    spr_here.start()
    spr_far = [
        remote(
            spread_ref, spr.at[pl.ds(24 - 24 * half, 8)], spr_send.at[1 + k],
            spr_recv.at[2 - half], beside, 4 * k + mem,
        )
        for k in range(2)
    ]
    for copy in spr_far:
        copy.start()

    def count_copy(j):
        to = lax.rem(ring + j, rings)
        return remote(cst.at[to], cra.at[ring], cnt_send.at[j], cnt_recv.at[ring], to, slot)

    loop(1, rings, lambda j: count_copy(j).start())

    edge_pair = 3 * half

    def permuted(to):
        row = lax.broadcasted_iota(jnp.int32, (160, 128), 0)
        lane = lax.broadcasted_iota(jnp.int32, (160, 128), 1)
        column = lax.rem(16 * to + row // 8 + 126, 128)
        level = lax.rem(row, 8)
        same = column == lane
        pick = jnp.concatenate(
            [jnp.where(same & (level == f), 1.0, 0.0).astype(BF16) for f in range(8)], axis=1
        )
        block = lax.dot_general(pick, v_ref[...], NT, preferred_element_type=F32).astype(BF16)
        for pair in range(4):
            snd[to, pair] = block[:, pair * 128 : (pair + 1) * 128]

    def main_copy(to):
        return remote(
            snd.at[to], rcv.at[pl.ds(1 + 4 * half, 4), mem], main_send.at[to],
            main_recv.at[slot], ring, to,
        )

    def halo_copy(to):
        return remote(
            snd.at[to, edge_pair], rcv.at[9 - 9 * half, mem], halo_send.at[to],
            halo_recv.at[1 - half, mem], beside, to,
        )

    def send_block(j):
        to = lax.rem(slot + j, 8)
        permuted(to)
        main_copy(to).start()
        halo_copy(to).start()

    loop(1, 8, send_block)
    permuted(slot)
    halo_copy(slot).start()
    own = pltpu.make_async_copy(
        snd.at[slot], rcv.at[pl.ds(1 + 4 * half, 4), mem], main_recv.at[slot]
    )
    own.start()

    def count_wait(j):
        frm = lax.rem(ring + j, rings)
        remote(cst.at[0], cra.at[frm], cnt_send.at[j], cnt_recv.at[frm], frm, slot).wait_recv()

    loop(1, rings, count_wait)
    total = cra[0]
    for r in range(1, rings):
        total = total + cra[r]
    crb[slot] = total

    def sum_copy(j):
        return remote(
            crb.at[slot], crb.at[slot], sum_send.at[j], sum_recv.at[slot], ring,
            lax.rem(slot + j, 8),
        )

    loop(1, 8, lambda j: sum_copy(j).start())

    spr_here.wait()
    for copy in spr_far:
        copy.wait_send()
    for k in range(2):
        remote(
            spread_ref, spr.at[pl.ds(24 * k, 8)], spr_send.at[0], spr_recv.at[1 + k],
            beside, mem,
        ).wait_recv()

    def spread_row(i):
        lane = lax.broadcasted_iota(jnp.int32, (20, 8, 128), 2)
        column = lax.rem(
            lax.broadcasted_iota(jnp.int32, (20, 8, 128), 0) + 16 * slot + 126, 128
        )
        values = jnp.where(lane == column, spr[i + 6][None], 0.0)
        coef[i] = jnp.broadcast_to(jnp.sum(values, axis=2, keepdims=True), (20, 8, 128))

    loop(0, 20, spread_row)

    def coef_row(i):
        coef_ref[i] = coef[i + 2, 2:18]

    loop(0, 16, coef_row)

    def sum_wait(j):
        frm = lax.rem(slot + j, 8)
        remote(crb.at[slot], crb.at[frm], sum_send.at[j], sum_recv.at[frm], ring, frm).wait_recv()

    loop(1, 8, sum_wait)
    counts = crb[0]
    for k in range(1, 8):
        counts = counts + crb[k]
    lane = lax.broadcasted_iota(jnp.int32, (8, 128), 1)
    for h in range(2):
        for c in range(2):
            mine = jnp.where(lane == h * 16 + 2 * slot + c, counts, 0.0)
            count = jnp.sum(mine, axis=1, keepdims=True)
            wt_ref[2 * h + c] = jnp.broadcast_to(count / (count + 16.0), (8, 128))

    own.wait()

    def main_wait(j):
        frm = lax.rem(slot + j, 8)
        remote(
            snd.at[0], rcv.at[pl.ds(1 + 4 * (frm // 4), 4), lax.rem(frm, 4)], main_send.at[0],
            main_recv.at[frm], ring, frm,
        ).wait_recv()

    loop(1, 8, main_wait)

    def halo_wait(k):
        remote(
            snd.at[0, 0], rcv.at[9 * (k // 4), lax.rem(k, 4)], halo_send.at[0],
            halo_recv.at[k // 4, lax.rem(k, 4)], beside, slot,
        ).wait_recv()

    loop(0, 8, halo_wait)

    def unshuffle(pair):
        low = lax.broadcasted_iota(jnp.int32, (160, 128), 1) < 64
        for mh in range(2):
            r0 = rcv[pair, 2 * mh].astype(F32)
            r1 = rcv[pair, 2 * mh + 1].astype(F32)
            even = jnp.where(low, r0, pltpu.roll(r1, 64, 1))
            odd = jnp.where(low, pltpu.roll(r0, 64, 1), r1)
            u0[mh, 2 * pair] = even.reshape(20, 8, 128)
            u0[mh, 2 * pair + 1] = odd.reshape(20, 8, 128)

    loop(0, 10, unshuffle)
    sx = sx_ref[...][None]
    sy = sy_ref[...][None]

    def first(x):
        s = coef[x, 1:19]
        for mh in range(2):
            u1[mh, x - 1] = rounded(
                stencil(
                    u0[mh, x, 1:19], u0[mh, x - 1, 1:19], u0[mh, x + 1, 1:19],
                    u0[mh, x, 0:18], u0[mh, x, 2:20], s, sx, sy,
                )
            )

    loop(1, 19, first)

    for h in range(2):

        def second(i):
            x = 8 * h + i + 1
            s = coef[x + 1, 2:18]
            prior = [
                rounded(
                    stencil(
                        u1[mh, x, 1:17], u1[mh, x - 1, 1:17], u1[mh, x + 1, 1:17],
                        u1[mh, x, 0:16], u1[mh, x, 2:18], s, sx, sy,
                    )
                )
                for mh in range(2)
            ]
            centre = jnp.sum(prior[0] + prior[1], axis=2, keepdims=True) * (1.0 / 256.0)
            centre = jnp.broadcast_to(centre, (16, 8, 128))
            for c in range(2):
                cols = slice(8 * c, 8 * c + 8)
                cen_ref[2 * h + c, i] = centre[cols].reshape(64, 128)
                for mh in range(2):
                    anom_ref[2 * h + c, i, :, mh * 128 : mh * 128 + 128] = (
                        (prior[mh][cols] - centre[cols]).reshape(64, 128).astype(BF16)
                    )

        loop(0, 8, second)

    row = lax.broadcasted_iota(jnp.int32, (128, 128), 0)
    col = lax.broadcasted_iota(jnp.int32, (128, 128), 1)

    def gram(p):
        a = anom_ref[p].reshape(512, 256)
        g = lax.dot_general(a, a, TN, preferred_element_type=F32) * (1.0 / 512.0)
        last = g[128:, 128:]
        gpk[p, 0:128] = g[:128, 128:]
        gpk[p, 128:256] = jnp.where(row >= col, g[:128, :128], last)
        diag = jnp.sum(jnp.where(row == col, last, 0.0), axis=0, keepdims=True)
        gpk[p, 256:264] = jnp.broadcast_to(diag, (8, 128))

    loop(0, 4, gram)
    copies = [
        remote(gpk.at[0:2], gbe, gram_send.at[0], gram_recv.at[0], above, slot),
        remote(gpk.at[2:4], gab, gram_send.at[1], gram_recv.at[1], below, slot),
    ]
    left = lax.rem(slot + 7, 8)
    right = lax.rem(slot + 1, 8)
    for h in range(2):
        copies.append(
            remote(gpk.at[2 * h], gri.at[h], gram_send.at[2 + h], gram_recv.at[2 + h], ring, left)
        )
        copies.append(
            remote(
                gpk.at[2 * h + 1], gle.at[h], gram_send.at[4 + h], gram_recv.at[4 + h], ring, right
            )
        )
    for copy in copies:
        copy.start()
    loop(1, rings, lambda j: count_copy(j).wait_send())
    loop(1, 8, lambda j: sum_copy(j).wait_send())
    loop(1, 8, lambda j: main_copy(lax.rem(slot + j, 8)).wait_send())
    loop(0, 8, lambda j: halo_copy(j).wait_send())
    for copy in copies:
        copy.wait()
    for h in range(2):
        for c in range(2):
            p = 2 * h + c
            up = gpk[c] if h else gab[c]
            down = gbe[c] if h else gpk[2 + c]
            lft = gpk[2 * h] if c else gle[h]
            rgt = gri[h] if c else gpk[2 * h + 1]
            avg_ref[p] = (2.0 * gpk[p] + up + down + lft + rgt) * (1.0 / 6.0)


def split(x):
    hi = x.astype(BF16)
    return hi, (x - hi.astype(F32)).astype(BF16)


def product(a, b):
    (ah, al), (bh, bl) = a, b
    return (
        jnp.dot(ah, bh, preferred_element_type=F32)
        + jnp.dot(ah, bl, preferred_element_type=F32)
        + jnp.dot(al, bh, preferred_element_type=F32)
    )


def analysis_kernel(anom_ref, cen_ref, avg_ref, wt_ref, out_ref, yh, yl, zh, zl):
    row = lax.broadcasted_iota(jnp.int32, (256, 256), 0)
    col = lax.broadcasted_iota(jnp.int32, (256, 256), 1)
    diagonal = row == col
    identity = jnp.where(diagonal, 1.0, 0.0)
    low = row[:128, :128] >= col[:128, :128]
    on = row[:128, :128] == col[:128, :128]

    def coefs(low_end, plain):
        alpha2 = jnp.where(plain, 1.0, 3.0 / (1.0 + low_end + low_end * low_end))
        alpha = jnp.sqrt(alpha2)
        reach = alpha * low_end
        after = 0.5 * reach * (3.0 - reach * reach)
        return 1.5 * alpha, 0.5 * alpha * alpha2, jnp.minimum(after, 1.0)

    ends, plains, scales = [], [], []
    for p in range(4):
        packed = avg_ref[p]
        upper_right = packed[0:128]
        both = packed[128:256]
        turned = both.T
        first = jnp.where(low, both, turned)
        last = jnp.where(on, jnp.broadcast_to(packed[256:257], (128, 128)), jnp.where(low, turned, both))
        averaged = jnp.concatenate(
            [
                jnp.concatenate([first, upper_right], axis=1),
                jnp.concatenate([upper_right.T, last], axis=1),
            ],
            axis=0,
        )
        system = identity + wt_ref[p, 0:1, 0:1] * averaged
        squares = jnp.sum(jnp.sum(system * system, axis=1, keepdims=True), axis=0, keepdims=True)
        norm = jnp.sqrt(squares)
        rows = jnp.max(
            jnp.sum(jnp.abs(system), axis=0, keepdims=True), axis=1, keepdims=True
        )
        plain = norm > PLAIN_NORM
        scale = jnp.where(plain, norm, jnp.minimum(norm, rows * 1.000001))
        start = system / scale
        low_end = jnp.where(plain, 0.0, jnp.sqrt(1.0 / scale) * 0.9999)
        a, b, after = coefs(low_end, plain)
        factor = a * identity - b * start
        y = product(split(start), split(factor))
        yh[p], yl[p] = split(y)
        zh[p], zl[p] = split(factor)
        ends.append(after)
        plains.append(plain)
        scales.append(scale)

    def some_left(ends, plains, k):
        left = jnp.zeros((1, 1), F32)
        for end, plain in zip(ends, plains):
            _, _, after = coefs(end, plain)
            todo = jnp.where(plain, jnp.where(k + 1 < NS_ITERS, 1.0, 0.0), jnp.where(1.0 - after > CONVERGED, 1.0, 0.0))
            left = jnp.maximum(left, todo)
        return jnp.max(left) > 0.5

    def body(carry):
        k, _, *ends = carry
        following = []
        for p in range(4):
            a, b, after = coefs(ends[p], plains[p])
            y = (yh[p], yl[p])
            z = (zh[p], zl[p])
            factor = split(a * identity - b * product(z, y))
            ny = product(y, factor)
            nz = product(factor, z)
            yh[p], yl[p] = split(ny)
            zh[p], zl[p] = split(nz)
            following.append(after)
        return (k + 1, some_left(following, plains, k + 1), *following)

    last_k, _, *ends = lax.while_loop(
        lambda carry: carry[1], body, (1, some_left(ends, plains, 1), *ends)
    )
    for p in range(4):
        a, b, _ = coefs(ends[p], plains[p])
        z = (zh[p], zl[p])
        factor = split(a * identity - b * product(z, (yh[p], yl[p])))
        inverse = product(factor, z)
        weights = (inverse / jnp.sqrt(scales[p])).astype(BF16)
        a = anom_ref[p].reshape(512, 256)
        update = jnp.dot(a, weights, preferred_element_type=F32)
        centre = cen_ref[p].reshape(512, 128)
        centre = jnp.concatenate([centre, centre], axis=1)
        h, c = p // 2, p % 2
        out_ref[8 * h : 8 * h + 8, 64 * c : 64 * c + 64, :] = (
            (centre + update).astype(BF16).reshape(8, 64, 256)
        )


def return_kernel(
    rings,
    f_ref,
    coef_ref,
    sx_ref,
    sy_ref,
    out_ref,
    g,
    west,
    east,
    from_above,
    from_below,
    from_left,
    from_right,
    snd,
    rcv,
    edge_send,
    edge_recv,
    main_send,
    main_recv,
    own_sem,
):
    ring, half, mem, slot = place()
    above = lax.rem(ring + rings - 1, rings)
    below = lax.rem(ring + 1, rings)
    left = lax.rem(slot + 7, 8)
    right = lax.rem(slot + 1, 8)
    barrier = pltpu.get_barrier_semaphore()
    loop(1, 8, lambda j: signal(barrier, ring, lax.rem(slot + j, 8)))
    signal(barrier, above, slot)
    signal(barrier, below, slot)

    def widen(x):
        plane = f_ref[x].astype(F32)
        for mh in range(2):
            g[mh, x + 1, 1:17] = plane[:, mh * 128 : mh * 128 + 128].reshape(16, 8, 128)

    loop(0, 16, widen)
    for mh in range(2):
        lanes = slice(mh * 128, mh * 128 + 128)
        west[:, lanes] = g[mh, 1:17, 1].reshape(128, 128).astype(BF16)
        east[:, lanes] = g[mh, 1:17, 16].reshape(128, 128).astype(BF16)
    pl.semaphore_wait(barrier, 9)
    edges = [
        remote(f_ref.at[0], from_below, edge_send.at[0], edge_recv.at[0], above, slot),
        remote(f_ref.at[15], from_above, edge_send.at[1], edge_recv.at[1], below, slot),
        remote(west, from_right, edge_send.at[2], edge_recv.at[2], ring, left),
        remote(east, from_left, edge_send.at[3], edge_recv.at[3], ring, right),
    ]
    for copy in edges:
        copy.start()
    for copy in edges:
        copy.wait()
    for mh in range(2):
        lanes = slice(mh * 128, mh * 128 + 128)
        g[mh, 0, 1:17] = from_above[:, lanes].astype(F32).reshape(16, 8, 128)
        g[mh, 17, 1:17] = from_below[:, lanes].astype(F32).reshape(16, 8, 128)
        g[mh, 1:17, 0] = from_left[:, lanes].astype(F32).reshape(16, 8, 128)
        g[mh, 1:17, 17] = from_right[:, lanes].astype(F32).reshape(16, 8, 128)
    sx = sx_ref[...][None]
    sy = sy_ref[...][None]
    low = lax.broadcasted_iota(jnp.int32, (128, 128), 1) < 64

    def main_copy(pair, to):
        return remote(
            snd.at[pair, to], rcv.at[pair, slot], main_send.at[pair, to],
            main_recv.at[pair, slot], ring, to,
        )

    def own_copy(pair):
        return pltpu.make_async_copy(snd.at[pair, slot], rcv.at[pair, slot], own_sem.at[pair])

    def send_pair(pair):
        for h in range(2):
            x = 8 * h + 2 * pair + 1
            for mh in range(2):
                even, odd = [
                    stencil(
                        g[mh, x + k, 1:17], g[mh, x + k - 1, 1:17], g[mh, x + k + 1, 1:17],
                        g[mh, x + k, 0:16], g[mh, x + k, 2:18], coef_ref[x + k - 1], sx, sy,
                    ).reshape(128, 128)
                    for k in range(2)
                ]
                snd[pair, 4 * h + 2 * mh] = jnp.where(low, even, pltpu.roll(odd, 64, 1)).astype(BF16)
                snd[pair, 4 * h + 2 * mh + 1] = jnp.where(low, pltpu.roll(even, 64, 1), odd).astype(BF16)
        loop(1, 8, lambda j: main_copy(pair, lax.rem(slot + j, 8)).start())
        own_copy(pair).start()

    loop(0, 4, send_pair)

    row = lax.broadcasted_iota(jnp.int32, (1024, 128), 0)
    lane = lax.broadcasted_iota(jnp.int32, (1024, 128), 1)
    same = row // 8 == lane
    level = lax.rem(row, 8)
    pick = jnp.concatenate(
        [jnp.where(same & (level == f), 1.0, 0.0).astype(BF16) for f in range(8)], axis=1
    )

    def receive_pair(pair):
        own_copy(pair).wait()

        def wait(j):
            frm = lax.rem(slot + j, 8)
            remote(
                snd.at[pair, frm], rcv.at[pair, frm], main_send.at[pair, frm],
                main_recv.at[pair, frm], ring, frm,
            ).wait_recv()

        loop(1, 8, wait)
        block = rcv[pair].reshape(1024, 128)
        result = lax.dot_general(block, pick, TN, preferred_element_type=F32).astype(BF16)
        out_ref[2 * pair] = result[:64]
        out_ref[2 * pair + 1] = result[64:]

    loop(0, 4, receive_pair)

    def finish(pair):
        loop(1, 8, lambda j: main_copy(pair, lax.rem(slot + j, 8)).wait_send())

    loop(0, 4, finish)


def vmem(count):
    return [pl.BlockSpec(memory_space=pltpu.VMEM)] * count


def local(member_collection, spreading_ratio, transport_ratio_row, transport_ratio_column, obs_patch):
    rings = lax.axis_size("tile") // 2
    DMA = pltpu.SemaphoreType.DMA
    state = jnp.transpose(member_collection, (2, 0, 1, 3)).reshape(512, 1024)
    spread = jnp.transpose(spreading_ratio, (1, 0, 2))
    sx = jnp.broadcast_to(transport_ratio_row[:, None], (8, 128))
    sy = jnp.broadcast_to(transport_ratio_column[:, None], (8, 128))
    obs = obs_patch.reshape(1, 256)

    def shape(dims, dtype=F32):
        return jax.ShapeDtypeStruct(dims, dtype)

    anom, cen, avg, wt, coef = pl.pallas_call(
        lambda *refs: forecast_kernel(rings, *refs),
        out_shape=[
            shape((4, 8, 64, 256), BF16),
            shape((4, 8, 64, 128)),
            shape((4, 264, 128)),
            shape((4, 8, 128)),
            shape((16, 16, 8, 128)),
        ],
        in_specs=vmem(5),
        out_specs=vmem(5),
        scratch_shapes=[
            pltpu.VMEM((8, 4, 160, 128), BF16),
            pltpu.VMEM((10, 4, 160, 128), BF16),
            pltpu.VMEM((2, 20, 20, 8, 128), F32),
            pltpu.VMEM((2, 18, 18, 8, 128), F32),
            pltpu.VMEM((20, 20, 8, 128), F32),
            pltpu.VMEM((32, 8, 128), F32),
            pltpu.VMEM((rings, 8, 128), F32),
            pltpu.VMEM((rings, 8, 128), F32),
            pltpu.VMEM((8, 8, 128), F32),
            pltpu.VMEM((4, 264, 128), F32),
            pltpu.VMEM((2, 264, 128), F32),
            pltpu.VMEM((2, 264, 128), F32),
            pltpu.VMEM((2, 264, 128), F32),
            pltpu.VMEM((2, 264, 128), F32),
            DMA((8,)),
            DMA((8,)),
            DMA((8,)),
            DMA((2, 4)),
            DMA((3,)),
            DMA((3,)),
            DMA((rings,)),
            DMA((rings,)),
            DMA((8,)),
            DMA((8,)),
            DMA((6,)),
            DMA((6,)),
        ],
        compiler_params=pltpu.CompilerParams(
            collective_id=0, has_side_effects=True, vmem_limit_bytes=VMEM_LIMIT
        ),
    )(state, spread, sx, sy, obs)

    field = pl.pallas_call(
        analysis_kernel,
        out_shape=shape((16, 128, 256), BF16),
        in_specs=vmem(4),
        out_specs=pl.BlockSpec(memory_space=pltpu.VMEM),
        scratch_shapes=[pltpu.VMEM((4, 256, 256), BF16)] * 4,
        compiler_params=pltpu.CompilerParams(vmem_limit_bytes=VMEM_LIMIT),
    )(anom, cen, avg, wt)

    out = pl.pallas_call(
        lambda *refs: return_kernel(rings, *refs),
        out_shape=shape((8, 64, 1024), BF16),
        in_specs=vmem(4),
        out_specs=pl.BlockSpec(memory_space=pltpu.VMEM),
        scratch_shapes=[
            pltpu.VMEM((2, 18, 18, 8, 128), F32),
            pltpu.VMEM((128, 256), BF16),
            pltpu.VMEM((128, 256), BF16),
            pltpu.VMEM((128, 256), BF16),
            pltpu.VMEM((128, 256), BF16),
            pltpu.VMEM((128, 256), BF16),
            pltpu.VMEM((128, 256), BF16),
            pltpu.VMEM((4, 8, 128, 128), BF16),
            pltpu.VMEM((4, 8, 128, 128), BF16),
            DMA((4,)),
            DMA((4,)),
            DMA((4, 8)),
            DMA((4, 8)),
            DMA((4,)),
        ],
        compiler_params=pltpu.CompilerParams(
            collective_id=1, has_side_effects=True, vmem_limit_bytes=VMEM_LIMIT
        ),
    )(field, coef, sx, sy)
    return jnp.transpose(out.reshape(8, 64, 8, 128), (1, 2, 0, 3))


def solution(mesh):
    placed = (P("mem", None, "tile", None), P(None, "tile", None), P(), P(), P(("mem", "tile")))
    return jax.shard_map(
        local, mesh=mesh, in_specs=placed, out_specs=P("mem", None, "tile", None), check_vma=False
    )
```

profile of v0, /device:TPU:1, one launch (start us, length us, event | category | flops | bytes accessed | tf_op | source)
XLA Modules:
  0.0 88.3 jit_solution(4266284427972001052)
XLA Ops:
  0.0 0.0 copy-start.1
  0.0 0.7 copy-done.1
  0.7 0.0 copy-start.2
  0.7 0.1 broadcast_in_dim.4.refs_2_
  0.7 0.6 copy-done.2
  1.3 0.1 broadcast_in_dim.5.refs_3_
  1.4 0.8 copy.16
  2.1 1.4 %copy.6 = bf16[8,64,8,128]{3,2,1,0:T(8,128)(2,1)S(1)} copy(bf16[8,64,8,128]{3,0,2,1:T(8,128)(2,1)} %bitcast.23) | data formatting | bytes 2097152 | tf_op jit(solution)/shard_map/transpose | solution.py:596
  3.5 1.2 %copy.14 = bf16[64,8,8,128]{3,1,2,0:T(8,128)(2,1)} copy(bf16[64,8,8,128]{3,2,1,0:T(8,128)(2,1)S(1)} %bitcast.22) | data formatting | bytes 2097152
  4.8 0.0 copy-start
  4.8 0.7 copy-done
  5.4 47.7 %shard_map.55 = (bf16[4,8,64,256]{3,2,1,0:T(8,128)(2,1)S(1)}, f32[4,8,64,128]{3,2,1,0:T(8,128)S(1)}, f32[4,264,128]{2,1,0:T(8,128)S(1)}, f32[4,8,128]{2,1,0:T(8,128)S(1)}, f32[16,16,8,128]{3,2,1,0:T(8,128)S(1)}) custom-call(bf16[512,1024]{1,0:T(8,128)(2,1)} %bitcast.20, f32[8,8,128]{2,1,0:T(8,128)S(1)} %bitcast.18, f32[8,128]{1,0:T(8,128)S(1)} %broadcast_in_dim.4.refs_2_, ...), custom_call_target="tpu_custom_call" | custom-call | tf_op jit(solution)/shard_map/pallas_call | solution.py:605
  53.1 8.1 %shard_map.56.refs_0_ = bf16[16,128,256]{2,1,0:T(8,128)(2,1)S(1)} custom-call(bf16[4,8,64,256]{3,2,1,0:T(8,128)(2,1)S(1)} %get-tuple-element.10.anom_ref, f32[4,8,64,128]{3,2,1,0:T(8,128)S(1)} %get-tuple-element.11.cen_ref, f32[4,264,128]{2,1,0:T(8,128)S(1)} %get-tuple-element.12.avg_ref, f32[4,8,128]{2,1,0:T(8,128)S(1)} %get-tuple-element.13.wt_ref), custom_call_target="tpu_custom_call" | custom-call | tf_op jit(solution)/shard_map/pallas_call | solution.py:649
  61.2 24.7 %shard_map.57 = bf16[8,64,1024]{2,1,0:T(8,128)(2,1)S(1)} custom-call(bf16[16,128,256]{2,1,0:T(8,128)(2,1)S(1)} %shard_map.56.refs_0_, f32[16,16,8,128]{3,2,1,0:T(8,128)S(1)} %get-tuple-element.14.refs_1_, f32[8,128]{1,0:T(8,128)S(1)} %broadcast_in_dim.4.refs_2_, f32[8,128]{1,0:T(8,128)S(1)} %broadcast_in_dim.5.refs_3_), custom_call_target="tpu_custom_call" | custom-call | tf_op jit(solution)/shard_map/pallas_call | solution.py:658
  85.9 0.3 copy.10
  86.2 2.2 %copy.15 = bf16[8,64,8,128]{3,0,2,1:T(8,128)(2,1)} copy(bf16[8,64,8,128]{3,2,1,0:T(8,128)(2,1)S(1)} %bitcast.21) | data formatting | bytes 2097152 | tf_op jit(solution)/shard_map/reshape | solution.py:683
Async XLA Ops:
  0.0 0.7 copy-start.1
  0.7 0.7 copy-start.2
  4.8 0.7 copy-start
where the time goes:
time: 88.6 us; the launch traced here: 88.3 us
  Pallas kernels  80.4 us (91%)
  local copies, waits for them, and re-layouts  7.89 us (9%)
    pallas_call x1, Pallas kernels, local(): pl.pallas_call(lambda *refs: forecast_kernel(rings, *refs), out_shape=[sh...  47.7 us
    pallas_call x1, Pallas kernels, local(): pl.pallas_call(lambda *refs: return_kernel(rings, *refs), out_shape=shape...  24.7 us
    pallas_call x1, Pallas kernels, local(): pl.pallas_call(analysis_kernel, out_shape=shape((16, 128, 256), BF16), in...  8.09 us
    unnamed x9, local copies, waits for them, and re-layouts  4.2 us
    reshape x1, local copies, waits for them, and re-layouts, local(): return jnp.transpose(out.reshape(8, 64, 8, 128), (1, 2, 0, 3))  2.2 us

commit v1 on v0

--- a/solution.py
+++ b/solution.py
@@ -61,16 +61,23 @@
 
 def forecast_kernel(
     rings,
-    v_ref,
-    spread_ref,
-    sx_ref,
-    sy_ref,
-    obs_ref,
+    u_hbm,
+    spread_hbm,
+    sx_hbm,
+    sy_hbm,
+    obs_hbm,
     anom_ref,
     cen_ref,
     avg_ref,
     wt_ref,
     coef_ref,
+    raw,
+    spread_in,
+    sx_in,
+    sy_in,
+    obs_in,
+    state,
+    picks,
     snd,
     rcv,
     u0,
@@ -85,8 +92,11 @@
     gbe,
     gle,
     gri,
-    main_send,
-    main_recv,
+    load_sem,
+    edge_send,
+    edge_recv,
+    rest_send,
+    rest_recv,
     halo_send,
     halo_recv,
     spr_send,
@@ -101,15 +111,126 @@
     ring, half, mem, slot = place()
     above = lax.rem(ring + rings - 1, rings)
     below = lax.rem(ring + 1, rings)
-    beside = lax.rem(ring + rings + 2 * half - 1, rings)
 
     barrier = pltpu.get_barrier_semaphore()
     loop(1, 8, lambda j: signal(barrier, ring, lax.rem(slot + j, 8)))
     loop(1, rings, lambda j: signal(barrier, lax.rem(ring + j, rings), slot))
-    loop(0, 4, lambda j: signal(barrier, above, 4 + j))
-    loop(0, 4, lambda j: signal(barrier, below, j))
-
-    obs = obs_ref[...]
+    loads = [
+        pltpu.make_async_copy(src, dst, load_sem.at[k])
+        for k, (src, dst) in enumerate(
+            [
+                (u_hbm, raw), (spread_hbm, spread_in), (sx_hbm, sx_in), (sy_hbm, sy_in),
+                (obs_hbm, obs_in),
+            ]
+        )
+    ]
+    for copy in loads:
+        copy.start()
+
+    k = lax.broadcasted_iota(jnp.int32, (512, 512), 1)
+    r = lax.broadcasted_iota(jnp.int32, (512, 512), 0)
+    turn = jnp.where(k == lax.rem(r, 64) * 8 + r // 64, 1.0, 0.0).astype(BF16)
+    loads[0].wait()
+    for f in range(8):
+        level = raw[:, f].astype(F32).reshape(512, 128).astype(BF16)
+        state[:, f * 128 : f * 128 + 128] = jnp.dot(
+            turn, level, preferred_element_type=F32
+        ).astype(BF16)
+
+    edge_pair = 3 * half
+    rest_pair = 1 - half
+    edge_rows = pl.ds(pl.multiple_of(128 * edge_pair, 128), 128)
+    rest_rows = pl.ds(pl.multiple_of(128 * rest_pair, 128), 384)
+
+    def edge_block(to):
+        row = lax.broadcasted_iota(jnp.int32, (160, 128), 0)
+        lane = lax.broadcasted_iota(jnp.int32, (160, 128), 1)
+        column = lax.rem(16 * to + row // 8 + 126, 128)
+        level = jnp.where(column == lane, lax.rem(row, 8), 8)
+        for f in range(8):
+            picks[to, :, f * 128 : f * 128 + 128] = jnp.where(level == f, 1.0, 0.0).astype(BF16)
+        snd[to, edge_pair] = lax.dot_general(
+            picks[to], state[edge_rows, :], NT, preferred_element_type=F32
+        ).astype(BF16)
+
+    def rest_block(to):
+        block = lax.dot_general(
+            picks[to], state[rest_rows, :], NT, preferred_element_type=F32
+        ).astype(BF16)
+        for pair in range(3):
+            snd[to, rest_pair + pair] = block[:, pair * 128 : (pair + 1) * 128]
+
+    def edge_copy(to):
+        return remote(
+            snd.at[to, edge_pair], rcv.at[1 + 7 * half, mem], edge_send.at[to],
+            edge_recv.at[slot], ring, to,
+        )
+
+    def rest_copy(to):
+        return remote(
+            snd.at[to, pl.ds(rest_pair, 3)], rcv.at[pl.ds(2 + 3 * half, 3), mem],
+            rest_send.at[to], rest_recv.at[slot], ring, to,
+        )
+
+    edge_block(lax.rem(slot + 1, 8))
+    pl.semaphore_wait(barrier, 7 + rings - 1)
+    edge_copy(lax.rem(slot + 1, 8)).start()
+
+    def send_edge(j):
+        to = lax.rem(slot + j, 8)
+        edge_block(to)
+        edge_copy(to).start()
+
+    loop(2, 8, send_edge)
+
+    def send_rest(j):
+        to = lax.rem(slot + j, 8)
+        rest_block(to)
+        rest_copy(to).start()
+
+    loop(1, 4, send_rest)
+    edge_block(slot)
+    own_edge = pltpu.make_async_copy(
+        snd.at[slot, edge_pair], rcv.at[1 + 7 * half, mem], edge_recv.at[slot]
+    )
+    own_edge.start()
+    loop(4, 8, send_rest)
+    rest_block(slot)
+    own_rest = pltpu.make_async_copy(
+        snd.at[slot, pl.ds(rest_pair, 3)], rcv.at[pl.ds(2 + 3 * half, 3), mem],
+        rest_recv.at[slot],
+    )
+    own_rest.start()
+
+    loads[1].wait()
+    mine = 8 + 8 * half
+    for x in range(8):
+        spr[mine + x] = spread_in[:, x, :]
+    spr_here = remote(
+        spr.at[pl.ds(mine, 8)], spr.at[pl.ds(mine, 8)], spr_send.at[0], spr_recv.at[0],
+        ring, (1 - half) * 4 + mem,
+    )
+    spr_here.start()
+
+    own_edge.wait()
+
+    def edge_wait(j):
+        frm = lax.rem(slot + j, 8)
+        remote(
+            snd.at[0, 0], rcv.at[1 + 7 * (frm // 4), lax.rem(frm, 4)], edge_send.at[frm],
+            edge_recv.at[frm], ring, frm,
+        ).wait_recv()
+
+    loop(1, 8, edge_wait)
+    halos = [
+        remote(rcv.at[1], rcv.at[9], halo_send.at[0], halo_recv.at[0], above, slot),
+        remote(rcv.at[8], rcv.at[0], halo_send.at[1], halo_recv.at[1], below, slot),
+    ]
+    for copy in halos:
+        copy.start()
+
+    loads[4].wait()
+    obs = obs_in[...]
     in_ring = lax.broadcasted_iota(jnp.int32, (rings, 256), 0) == obs // 32
     in_patch = lax.broadcasted_iota(jnp.int32, (128, 256), 0) == lax.rem(obs, 32)
     tally = lax.dot_general(
@@ -119,98 +240,25 @@
     for r in range(rings):
         cst[r] = jnp.broadcast_to(tally[r : r + 1, :], (8, 128))
     cra[ring] = cst[ring]
-    spr[pl.ds(8 + 8 * half, 8)] = spread_ref[...]
-
-    pl.semaphore_wait(barrier, 7 + rings - 1 + 8)
-
-    spr_here = remote(
-        spread_ref, spr.at[pl.ds(8 + 8 * half, 8)], spr_send.at[0], spr_recv.at[0],
+
+    def count_copy(j):
+        to = lax.rem(ring + j, rings)
+        return remote(cst.at[to], cra.at[ring], cnt_send.at[j], cnt_recv.at[ring], to, slot)
+
+    loop(1, rings, lambda j: count_copy(j).start())
+
+    spr_here.wait_send()
+    other = 16 - 8 * half
+    remote(
+        spr.at[pl.ds(other, 8)], spr.at[pl.ds(other, 8)], spr_send.at[0], spr_recv.at[0],
         ring, (1 - half) * 4 + mem,
-    )
-    spr_here.start()
+    ).wait_recv()
     spr_far = [
-        remote(
-            spread_ref, spr.at[pl.ds(24 - 24 * half, 8)], spr_send.at[1 + k],
-            spr_recv.at[2 - half], beside, 4 * k + mem,
-        )
-        for k in range(2)
+        remote(spr.at[8:10], spr.at[24:26], spr_send.at[1], spr_recv.at[1], above, slot),
+        remote(spr.at[22:24], spr.at[6:8], spr_send.at[2], spr_recv.at[2], below, slot),
     ]
     for copy in spr_far:
         copy.start()
-
-    def count_copy(j):
-        to = lax.rem(ring + j, rings)
-        return remote(cst.at[to], cra.at[ring], cnt_send.at[j], cnt_recv.at[ring], to, slot)
-
-    loop(1, rings, lambda j: count_copy(j).start())
-
-    edge_pair = 3 * half
-
-    def permuted(to):
-        row = lax.broadcasted_iota(jnp.int32, (160, 128), 0)
-        lane = lax.broadcasted_iota(jnp.int32, (160, 128), 1)
-        column = lax.rem(16 * to + row // 8 + 126, 128)
-        level = lax.rem(row, 8)
-        same = column == lane
-        pick = jnp.concatenate(
-            [jnp.where(same & (level == f), 1.0, 0.0).astype(BF16) for f in range(8)], axis=1
-        )
-        block = lax.dot_general(pick, v_ref[...], NT, preferred_element_type=F32).astype(BF16)
-        for pair in range(4):
-            snd[to, pair] = block[:, pair * 128 : (pair + 1) * 128]
-
-    def main_copy(to):
-        return remote(
-            snd.at[to], rcv.at[pl.ds(1 + 4 * half, 4), mem], main_send.at[to],
-            main_recv.at[slot], ring, to,
-        )
-
-    def halo_copy(to):
-        return remote(
-            snd.at[to, edge_pair], rcv.at[9 - 9 * half, mem], halo_send.at[to],
-            halo_recv.at[1 - half, mem], beside, to,
-        )
-
-    def send_block(j):
-        to = lax.rem(slot + j, 8)
-        permuted(to)
-        main_copy(to).start()
-        halo_copy(to).start()
-
-    loop(1, 8, send_block)
-    permuted(slot)
-    halo_copy(slot).start()
-    own = pltpu.make_async_copy(
-        snd.at[slot], rcv.at[pl.ds(1 + 4 * half, 4), mem], main_recv.at[slot]
-    )
-    own.start()
-
-    def count_wait(j):
-        frm = lax.rem(ring + j, rings)
-        remote(cst.at[0], cra.at[frm], cnt_send.at[j], cnt_recv.at[frm], frm, slot).wait_recv()
-
-    loop(1, rings, count_wait)
-    total = cra[0]
-    for r in range(1, rings):
-        total = total + cra[r]
-    crb[slot] = total
-
-    def sum_copy(j):
-        return remote(
-            crb.at[slot], crb.at[slot], sum_send.at[j], sum_recv.at[slot], ring,
-            lax.rem(slot + j, 8),
-        )
-
-    loop(1, 8, lambda j: sum_copy(j).start())
-
-    spr_here.wait()
-    for copy in spr_far:
-        copy.wait_send()
-    for k in range(2):
-        remote(
-            spread_ref, spr.at[pl.ds(24 * k, 8)], spr_send.at[0], spr_recv.at[1 + k],
-            beside, mem,
-        ).wait_recv()
 
     def spread_row(i):
         lane = lax.broadcasted_iota(jnp.int32, (20, 8, 128), 2)
@@ -220,46 +268,24 @@
         values = jnp.where(lane == column, spr[i + 6][None], 0.0)
         coef[i] = jnp.broadcast_to(jnp.sum(values, axis=2, keepdims=True), (20, 8, 128))
 
-    loop(0, 20, spread_row)
+    loop(2, 18, spread_row)
 
     def coef_row(i):
         coef_ref[i] = coef[i + 2, 2:18]
 
     loop(0, 16, coef_row)
-
-    def sum_wait(j):
-        frm = lax.rem(slot + j, 8)
-        remote(crb.at[slot], crb.at[frm], sum_send.at[j], sum_recv.at[frm], ring, frm).wait_recv()
-
-    loop(1, 8, sum_wait)
-    counts = crb[0]
-    for k in range(1, 8):
-        counts = counts + crb[k]
-    lane = lax.broadcasted_iota(jnp.int32, (8, 128), 1)
-    for h in range(2):
-        for c in range(2):
-            mine = jnp.where(lane == h * 16 + 2 * slot + c, counts, 0.0)
-            count = jnp.sum(mine, axis=1, keepdims=True)
-            wt_ref[2 * h + c] = jnp.broadcast_to(count / (count + 16.0), (8, 128))
-
-    own.wait()
-
-    def main_wait(j):
-        frm = lax.rem(slot + j, 8)
-        remote(
-            snd.at[0], rcv.at[pl.ds(1 + 4 * (frm // 4), 4), lax.rem(frm, 4)], main_send.at[0],
-            main_recv.at[frm], ring, frm,
-        ).wait_recv()
-
-    loop(1, 8, main_wait)
-
-    def halo_wait(k):
-        remote(
-            snd.at[0, 0], rcv.at[9 * (k // 4), lax.rem(k, 4)], halo_send.at[0],
-            halo_recv.at[k // 4, lax.rem(k, 4)], beside, slot,
-        ).wait_recv()
-
-    loop(0, 8, halo_wait)
+    for copy in spr_far:
+        copy.wait()
+    for i in (0, 1, 18, 19):
+        spread_row(i)
+    loads[2].wait()
+    loads[3].wait()
+    sublane = lax.broadcasted_iota(jnp.int32, (8, 128), 0)
+    for k, ref in enumerate((sx_in, sy_in)):
+        speed = jnp.zeros((8, 128), F32)
+        for f in range(8):
+            speed = jnp.where(sublane == f, ref[f], speed)
+        wt_ref[4 + k] = speed
 
     def unshuffle(pair):
         low = lax.broadcasted_iota(jnp.int32, (160, 128), 1) < 64
@@ -271,9 +297,26 @@
             u0[mh, 2 * pair] = even.reshape(20, 8, 128)
             u0[mh, 2 * pair + 1] = odd.reshape(20, 8, 128)
 
-    loop(0, 10, unshuffle)
-    sx = sx_ref[...][None]
-    sy = sy_ref[...][None]
+    unshuffle(1)
+    unshuffle(8)
+    for copy in halos:
+        copy.wait()
+    unshuffle(0)
+    unshuffle(9)
+
+    own_rest.wait()
+
+    def rest_wait(j):
+        frm = lax.rem(slot + j, 8)
+        remote(
+            snd.at[0, 0:3], rcv.at[pl.ds(2 + 3 * (frm // 4), 3), lax.rem(frm, 4)],
+            rest_send.at[frm], rest_recv.at[frm], ring, frm,
+        ).wait_recv()
+
+    loop(1, 8, rest_wait)
+    loop(2, 8, unshuffle)
+    sx = wt_ref[4][None]
+    sy = wt_ref[5][None]
 
     def first(x):
         s = coef[x, 1:19]
@@ -287,70 +330,101 @@
 
     loop(1, 19, first)
 
-    for h in range(2):
-
-        def second(i):
-            x = 8 * h + i + 1
-            s = coef[x + 1, 2:18]
-            prior = [
-                rounded(
-                    stencil(
-                        u1[mh, x, 1:17], u1[mh, x - 1, 1:17], u1[mh, x + 1, 1:17],
-                        u1[mh, x, 0:16], u1[mh, x, 2:18], s, sx, sy,
-                    )
-                )
-                for mh in range(2)
-            ]
-            centre = jnp.sum(prior[0] + prior[1], axis=2, keepdims=True) * (1.0 / 256.0)
-            centre = jnp.broadcast_to(centre, (16, 8, 128))
-            for c in range(2):
-                cols = slice(8 * c, 8 * c + 8)
-                cen_ref[2 * h + c, i] = centre[cols].reshape(64, 128)
-                for mh in range(2):
-                    anom_ref[2 * h + c, i, :, mh * 128 : mh * 128 + 128] = (
-                        (prior[mh][cols] - centre[cols]).reshape(64, 128).astype(BF16)
-                    )
-
-        loop(0, 8, second)
+    def count_wait(j):
+        frm = lax.rem(ring + j, rings)
+        remote(cst.at[0], cra.at[frm], cnt_send.at[j], cnt_recv.at[frm], frm, slot).wait_recv()
+
+    loop(1, rings, count_wait)
+    total = cra[0]
+    for r in range(1, rings):
+        total = total + cra[r]
+    crb[slot] = total
+
+    def sum_copy(j):
+        return remote(
+            crb.at[slot], crb.at[slot], sum_send.at[j], sum_recv.at[slot], ring,
+            lax.rem(slot + j, 8),
+        )
+
+    loop(1, 8, lambda j: sum_copy(j).start())
 
     row = lax.broadcasted_iota(jnp.int32, (128, 128), 0)
     col = lax.broadcasted_iota(jnp.int32, (128, 128), 1)
-
-    def gram(p):
-        a = anom_ref[p].reshape(512, 256)
-        g = lax.dot_general(a, a, TN, preferred_element_type=F32) * (1.0 / 512.0)
-        last = g[128:, 128:]
-        gpk[p, 0:128] = g[:128, 128:]
-        gpk[p, 128:256] = jnp.where(row >= col, g[:128, :128], last)
-        diag = jnp.sum(jnp.where(row == col, last, 0.0), axis=0, keepdims=True)
-        gpk[p, 256:264] = jnp.broadcast_to(diag, (8, 128))
-
-    loop(0, 4, gram)
-    copies = [
-        remote(gpk.at[0:2], gbe, gram_send.at[0], gram_recv.at[0], above, slot),
-        remote(gpk.at[2:4], gab, gram_send.at[1], gram_recv.at[1], below, slot),
-    ]
     left = lax.rem(slot + 7, 8)
     right = lax.rem(slot + 1, 8)
+    copies = []
+    for c in range(2):
+        for h in range(2):
+            p = 2 * h + c
+
+            def second(i, h=h, c=c, p=p):
+                x = 8 * h + i + 1
+                y = 8 * c + 1
+                s = coef[x + 1, y + 1 : y + 9]
+                prior = [
+                    rounded(
+                        stencil(
+                            u1[mh, x, y : y + 8], u1[mh, x - 1, y : y + 8],
+                            u1[mh, x + 1, y : y + 8], u1[mh, x, y - 1 : y + 7],
+                            u1[mh, x, y + 1 : y + 9], s, sx, sy,
+                        )
+                    )
+                    for mh in range(2)
+                ]
+                centre = jnp.sum(prior[0] + prior[1], axis=2, keepdims=True) * (1.0 / 256.0)
+                centre = jnp.broadcast_to(centre, (8, 8, 128))
+                cen_ref[p, i] = centre.reshape(64, 128)
+                for mh in range(2):
+                    anom_ref[p, i, :, mh * 128 : mh * 128 + 128] = (
+                        (prior[mh] - centre).reshape(64, 128).astype(BF16)
+                    )
+
+            loop(0, 8, second)
+            a = anom_ref[p].reshape(512, 256)
+            g = lax.dot_general(a, a, TN, preferred_element_type=F32) * (1.0 / 512.0)
+            last = g[128:, 128:]
+            gpk[p, 0:128] = g[:128, 128:]
+            gpk[p, 128:256] = jnp.where(row >= col, g[:128, :128], last)
+            diag = jnp.sum(jnp.where(row == col, last, 0.0), axis=0, keepdims=True)
+            gpk[p, 256:264] = jnp.broadcast_to(diag, (8, 128))
+            vertical = (gab, below) if h else (gbe, above)
+            sideways = (gle, right) if c else (gri, left)
+            pair = [
+                remote(
+                    gpk.at[p], vertical[0].at[c], gram_send.at[2 * p], gram_recv.at[2 * p],
+                    vertical[1], slot,
+                ),
+                remote(
+                    gpk.at[p], sideways[0].at[h], gram_send.at[2 * p + 1],
+                    gram_recv.at[2 * p + 1], ring, sideways[1],
+                ),
+            ]
+            for copy in pair:
+                copy.start()
+            copies += pair
+
+    def sum_wait(j):
+        frm = lax.rem(slot + j, 8)
+        remote(crb.at[slot], crb.at[frm], sum_send.at[j], sum_recv.at[frm], ring, frm).wait_recv()
+
+    loop(1, 8, sum_wait)
+    counts = crb[0]
+    for k in range(1, 8):
+        counts = counts + crb[k]
+    lane = lax.broadcasted_iota(jnp.int32, (8, 128), 1)
     for h in range(2):
-        copies.append(
-            remote(gpk.at[2 * h], gri.at[h], gram_send.at[2 + h], gram_recv.at[2 + h], ring, left)
-        )
-        copies.append(
-            remote(
-                gpk.at[2 * h + 1], gle.at[h], gram_send.at[4 + h], gram_recv.at[4 + h], ring, right
-            )
-        )
-    for copy in copies:
-        copy.start()
+        for c in range(2):
+            chosen = jnp.where(lane == h * 16 + 2 * slot + c, counts, 0.0)
+            count = jnp.sum(chosen, axis=1, keepdims=True)
+            wt_ref[2 * h + c] = jnp.broadcast_to(count / (count + 16.0), (8, 128))
     loop(1, rings, lambda j: count_copy(j).wait_send())
     loop(1, 8, lambda j: sum_copy(j).wait_send())
-    loop(1, 8, lambda j: main_copy(lax.rem(slot + j, 8)).wait_send())
-    loop(0, 8, lambda j: halo_copy(j).wait_send())
+    loop(1, 8, lambda j: edge_copy(lax.rem(slot + j, 8)).wait_send())
+    loop(1, 8, lambda j: rest_copy(lax.rem(slot + j, 8)).wait_send())
     for copy in copies:
         copy.wait()
-    for h in range(2):
-        for c in range(2):
+    for c in range(2):
+        for h in range(2):
             p = 2 * h + c
             up = gpk[c] if h else gab[c]
             down = gbe[c] if h else gpk[2 + c]
@@ -468,8 +542,7 @@
     rings,
     f_ref,
     coef_ref,
-    sx_ref,
-    sy_ref,
+    wt_ref,
     out_ref,
     g,
     west,
@@ -523,8 +596,8 @@
         g[mh, 17, 1:17] = from_below[:, lanes].astype(F32).reshape(16, 8, 128)
         g[mh, 1:17, 0] = from_left[:, lanes].astype(F32).reshape(16, 8, 128)
         g[mh, 1:17, 17] = from_right[:, lanes].astype(F32).reshape(16, 8, 128)
-    sx = sx_ref[...][None]
-    sy = sy_ref[...][None]
+    sx = wt_ref[4][None]
+    sy = wt_ref[5][None]
     low = lax.broadcasted_iota(jnp.int32, (128, 128), 1) < 64
 
     def main_copy(pair, to):
@@ -593,10 +666,6 @@
 def local(member_collection, spreading_ratio, transport_ratio_row, transport_ratio_column, obs_patch):
     rings = lax.axis_size("tile") // 2
     DMA = pltpu.SemaphoreType.DMA
-    state = jnp.transpose(member_collection, (2, 0, 1, 3)).reshape(512, 1024)
-    spread = jnp.transpose(spreading_ratio, (1, 0, 2))
-    sx = jnp.broadcast_to(transport_ratio_row[:, None], (8, 128))
-    sy = jnp.broadcast_to(transport_ratio_column[:, None], (8, 128))
     obs = obs_patch.reshape(1, 256)
 
     def shape(dims, dtype=F32):
@@ -608,12 +677,19 @@
             shape((4, 8, 64, 256), BF16),
             shape((4, 8, 64, 128)),
             shape((4, 264, 128)),
-            shape((4, 8, 128)),
+            shape((6, 8, 128)),
             shape((16, 16, 8, 128)),
         ],
-        in_specs=vmem(5),
+        in_specs=[pl.BlockSpec(memory_space=pltpu.HBM)] * 5,
         out_specs=vmem(5),
         scratch_shapes=[
+            pltpu.VMEM((64, 8, 8, 128), BF16),
+            pltpu.VMEM((8, 8, 128), F32),
+            pltpu.SMEM((8,), F32),
+            pltpu.SMEM((8,), F32),
+            pltpu.VMEM((1, 256), jnp.int32),
+            pltpu.VMEM((512, 1024), BF16),
+            pltpu.VMEM((8, 160, 1024), BF16),
             pltpu.VMEM((8, 4, 160, 128), BF16),
             pltpu.VMEM((10, 4, 160, 128), BF16),
             pltpu.VMEM((2, 20, 20, 8, 128), F32),
@@ -628,23 +704,26 @@
             pltpu.VMEM((2, 264, 128), F32),
             pltpu.VMEM((2, 264, 128), F32),
             pltpu.VMEM((2, 264, 128), F32),
+            DMA((5,)),
             DMA((8,)),
             DMA((8,)),
             DMA((8,)),
-            DMA((2, 4)),
+            DMA((8,)),
+            DMA((2,)),
+            DMA((2,)),
             DMA((3,)),
             DMA((3,)),
             DMA((rings,)),
             DMA((rings,)),
             DMA((8,)),
             DMA((8,)),
-            DMA((6,)),
-            DMA((6,)),
+            DMA((8,)),
+            DMA((8,)),
         ],
         compiler_params=pltpu.CompilerParams(
             collective_id=0, has_side_effects=True, vmem_limit_bytes=VMEM_LIMIT
         ),
-    )(state, spread, sx, sy, obs)
+    )(member_collection, spreading_ratio, transport_ratio_row, transport_ratio_column, obs)
 
     field = pl.pallas_call(
         analysis_kernel,
@@ -658,7 +737,7 @@
     out = pl.pallas_call(
         lambda *refs: return_kernel(rings, *refs),
         out_shape=shape((8, 64, 1024), BF16),
-        in_specs=vmem(4),
+        in_specs=vmem(3),
         out_specs=pl.BlockSpec(memory_space=pltpu.VMEM),
         scratch_shapes=[
             pltpu.VMEM((2, 18, 18, 8, 128), F32),
@@ -679,7 +758,7 @@
         compiler_params=pltpu.CompilerParams(
             collective_id=1, has_side_effects=True, vmem_limit_bytes=VMEM_LIMIT
         ),
-    )(field, coef, sx, sy)
+    )(field, coef, wt)
     return jnp.transpose(out.reshape(8, 64, 8, 128), (1, 2, 0, 3))
 
 

time: 88.6 us -> 79.7 us (0.90)
  Pallas kernels: 80.4 us -> 74.9 us
  local copies, waits for them, and re-layouts: 7.89 us -> 4.55 us
    pallas_call x1, Pallas kernels: 47.7 us -> 42.7 us  [local(): pl.pallas_call(lambda *refs: forecast_kernel(rings, *refs), out_shape=[sh...]
    unnamed x9, local copies, waits for them, and re-layouts: 4.2 us -> 2.36 us
    transpose x1 -> x0, local copies, waits for them, and re-layouts: 1.36 us -> none  [local(): state = jnp.transpose(member_collection, (2, 0, 1, 3)).reshape(512, 1024)]
where the time goes in v1:
time: 79.7 us; the launch traced here: 79.5 us
  Pallas kernels  74.9 us (94%)
  local copies, waits for them, and re-layouts  4.55 us (6%)
    pallas_call x1, Pallas kernels, local(): pl.pallas_call(lambda *refs: forecast_kernel(rings, *refs), out_shape=[sh...  42.7 us
    pallas_call x1, Pallas kernels, local(): pl.pallas_call(lambda *refs: return_kernel(rings, *refs), out_shape=shape...  23.9 us
    pallas_call x1, Pallas kernels, local(): pl.pallas_call(analysis_kernel, out_shape=shape((16, 128, 256), BF16), in...  8.26 us
    unnamed x9, local copies, waits for them, and re-layouts  2.36 us
    reshape x1, local copies, waits for them, and re-layouts, local(): return jnp.transpose(out.reshape(8, 64, 8, 128), (1, 2, 0, 3))  2.2 us

profile of v1, /device:TPU:1, one launch (start us, length us, event | category | flops | bytes accessed | tf_op | source)
XLA Modules:
  0.0 79.5 jit_solution(12921843579772653294)
XLA Ops:
  0.0 0.0 copy-start.1
  0.0 0.0 copy-start.2
  0.0 0.7 copy-done.1
  0.7 0.0 copy-done.2
  0.7 0.0 copy-start
  0.7 0.8 copy-done
  1.4 0.0 copy-start.3
  1.4 0.7 copy-done.3
  2.1 42.7 %shard_map.55 = (bf16[4,8,64,256]{3,2,1,0:T(8,128)(2,1)S(1)}, f32[4,8,64,128]{3,2,1,0:T(8,128)S(1)}, f32[4,264,128]{2,1,0:T(8,128)S(1)}, f32[6,8,128]{2,1,0:T(8,128)S(1)}, f32[16,16,8,128]{3,2,1,0:T(8,128)S(1)}) custom-call(bf16[64,8,8,128]{3,2,1,0:T(8,128)(2,1)} %refs_0_.1, f32[8,8,128]{2,1,0:T(8,128)S(1)} %copy-done, f32[8]{0:T(128)S(1)} %copy-done.2, ...), custom_call_target="tpu_custom_call" | custom-call | tf_op jit(solution)/shard_map/pallas_call | solution.py:674
  44.8 8.3 %shard_map.56.refs_0_ = bf16[16,128,256]{2,1,0:T(8,128)(2,1)S(1)} custom-call(bf16[4,8,64,256]{3,2,1,0:T(8,128)(2,1)S(1)} %get-tuple-element.10.anom_ref, f32[4,8,64,128]{3,2,1,0:T(8,128)S(1)} %get-tuple-element.11.cen_ref, f32[4,264,128]{2,1,0:T(8,128)S(1)} %get-tuple-element.12.avg_ref, f32[6,8,128]{2,1,0:T(8,128)S(1)} %get-tuple-element.13.wt_ref.refs_2_), custom_call_target="tpu_custom_call" | custom-call | tf_op jit(solution)/shard_map/pallas_call | solution.py:728
  53.1 23.9 %shard_map.57 = bf16[8,64,1024]{2,1,0:T(8,128)(2,1)S(1)} custom-call(bf16[16,128,256]{2,1,0:T(8,128)(2,1)S(1)} %shard_map.56.refs_0_, f32[16,16,8,128]{3,2,1,0:T(8,128)S(1)} %get-tuple-element.14.refs_1_, f32[6,8,128]{2,1,0:T(8,128)S(1)} %get-tuple-element.13.wt_ref.refs_2_), custom_call_target="tpu_custom_call" | custom-call | tf_op jit(solution)/shard_map/pallas_call | solution.py:737
  77.0 0.3 copy.7
  77.3 2.2 %copy.9 = bf16[8,64,8,128]{3,0,2,1:T(8,128)(2,1)} copy(bf16[8,64,8,128]{3,2,1,0:T(8,128)(2,1)S(1)} %bitcast.10) | data formatting | bytes 2097152 | tf_op jit(solution)/shard_map/reshape | solution.py:762
Async XLA Ops:
  0.0 0.7 copy-start.1
  0.0 0.7 copy-start.2
  0.7 0.8 copy-start
  1.4 0.7 copy-start.3

commit v2 on v1

--- a/solution.py
+++ b/solution.py
@@ -11,7 +11,7 @@
 VMEM_LIMIT = 50 * 1024 * 1024
 NS_ITERS = 14
 PLAIN_NORM = 2500.0
-CONVERGED = 1e-6
+CONVERGED = 1e-5
 NT = (((1,), (1,)), ((), ()))
 TN = (((0,), (0,)), ((), ()))
 
@@ -76,9 +76,10 @@
     sx_in,
     sy_in,
     obs_in,
+    flat,
     state,
-    picks,
-    snd,
+    pick,
+    wide,
     rcv,
     u0,
     u1,
@@ -127,77 +128,77 @@
     for copy in loads:
         copy.start()
 
-    k = lax.broadcasted_iota(jnp.int32, (512, 512), 1)
-    r = lax.broadcasted_iota(jnp.int32, (512, 512), 0)
-    turn = jnp.where(k == lax.rem(r, 64) * 8 + r // 64, 1.0, 0.0).astype(BF16)
+    def pick_rows(i):
+        row = lax.broadcasted_iota(jnp.int32, (128, 128), 0) + 128 * i
+        lane = lax.broadcasted_iota(jnp.int32, (128, 128), 1)
+        level = jnp.where(row // 8 == lane, lax.rem(row, 8), 8)
+        rows = pl.ds(pl.multiple_of(128 * i, 128), 128)
+        for f in range(8):
+            pick[rows, f * 128 : f * 128 + 128] = jnp.where(level == f, 1.0, 0.0).astype(BF16)
+
+    loop(0, 8, pick_rows)
+
+    edge_pair = 3 * half
+    rest_pair = 1 - half
+
+    def turned(first, count):
+        k = lax.broadcasted_iota(jnp.int32, (128 * count, 512), 1)
+        r = lax.broadcasted_iota(jnp.int32, (128 * count, 512), 0) + 128 * first
+        turn = jnp.where(k == lax.rem(r, 64) * 8 + r // 64, 1.0, 0.0).astype(BF16)
+        return jnp.dot(turn, flat[...], preferred_element_type=F32).astype(BF16)
+
+    def store_pair(pair, block):
+        wide[pair, 16:1040] = block
+        wide[pair, 0:16] = block[1008:1024]
+        wide[pair, 1040:1056] = block[0:16]
+
     loads[0].wait()
     for f in range(8):
-        level = raw[:, f].astype(F32).reshape(512, 128).astype(BF16)
-        state[:, f * 128 : f * 128 + 128] = jnp.dot(
-            turn, level, preferred_element_type=F32
-        ).astype(BF16)
-
-    edge_pair = 3 * half
-    rest_pair = 1 - half
-    edge_rows = pl.ds(pl.multiple_of(128 * edge_pair, 128), 128)
-    rest_rows = pl.ds(pl.multiple_of(128 * rest_pair, 128), 384)
-
-    def edge_block(to):
-        row = lax.broadcasted_iota(jnp.int32, (160, 128), 0)
-        lane = lax.broadcasted_iota(jnp.int32, (160, 128), 1)
-        column = lax.rem(16 * to + row // 8 + 126, 128)
-        level = jnp.where(column == lane, lax.rem(row, 8), 8)
-        for f in range(8):
-            picks[to, :, f * 128 : f * 128 + 128] = jnp.where(level == f, 1.0, 0.0).astype(BF16)
-        snd[to, edge_pair] = lax.dot_general(
-            picks[to], state[edge_rows, :], NT, preferred_element_type=F32
-        ).astype(BF16)
-
-    def rest_block(to):
+        flat[:, f * 128 : f * 128 + 128] = raw[:, f].astype(F32).reshape(512, 128).astype(BF16)
+    state[0:128] = turned(edge_pair, 1)
+    store_pair(
+        edge_pair,
+        lax.dot_general(pick[...], state[0:128], NT, preferred_element_type=F32).astype(BF16),
+    )
+
+    def edge_copy(to):
+        return remote(
+            wide.at[edge_pair, pl.ds(pl.multiple_of(128 * to, 128), 160)],
+            rcv.at[1 + 7 * half, mem], edge_send.at[to], edge_recv.at[slot], ring, to,
+        )
+
+    def rest_copy(to):
+        return remote(
+            wide.at[pl.ds(rest_pair, 3), pl.ds(pl.multiple_of(128 * to, 128), 160)],
+            rcv.at[pl.ds(2 + 3 * half, 3), mem], rest_send.at[to], rest_recv.at[slot], ring, to,
+        )
+
+    pl.semaphore_wait(barrier, 7 + rings - 1)
+    loop(1, 8, lambda j: edge_copy(lax.rem(slot + j, 8)).start())
+    own_rows = pl.ds(pl.multiple_of(128 * slot, 128), 160)
+    own_edge = pltpu.make_async_copy(
+        wide.at[edge_pair, own_rows], rcv.at[1 + 7 * half, mem], edge_recv.at[slot]
+    )
+    own_edge.start()
+    state[128:512] = turned(rest_pair, 3)
+
+    def rest_rows(i):
+        rows = pl.ds(pl.multiple_of(128 * i, 128), 128)
         block = lax.dot_general(
-            picks[to], state[rest_rows, :], NT, preferred_element_type=F32
+            pick[rows, :], state[128:512], NT, preferred_element_type=F32
         ).astype(BF16)
         for pair in range(3):
-            snd[to, rest_pair + pair] = block[:, pair * 128 : (pair + 1) * 128]
-
-    def edge_copy(to):
-        return remote(
-            snd.at[to, edge_pair], rcv.at[1 + 7 * half, mem], edge_send.at[to],
-            edge_recv.at[slot], ring, to,
-        )
-
-    def rest_copy(to):
-        return remote(
-            snd.at[to, pl.ds(rest_pair, 3)], rcv.at[pl.ds(2 + 3 * half, 3), mem],
-            rest_send.at[to], rest_recv.at[slot], ring, to,
-        )
-
-    edge_block(lax.rem(slot + 1, 8))
-    pl.semaphore_wait(barrier, 7 + rings - 1)
-    edge_copy(lax.rem(slot + 1, 8)).start()
-
-    def send_edge(j):
-        to = lax.rem(slot + j, 8)
-        edge_block(to)
-        edge_copy(to).start()
-
-    loop(2, 8, send_edge)
-
-    def send_rest(j):
-        to = lax.rem(slot + j, 8)
-        rest_block(to)
-        rest_copy(to).start()
-
-    loop(1, 4, send_rest)
-    edge_block(slot)
-    own_edge = pltpu.make_async_copy(
-        snd.at[slot, edge_pair], rcv.at[1 + 7 * half, mem], edge_recv.at[slot]
-    )
-    own_edge.start()
-    loop(4, 8, send_rest)
-    rest_block(slot)
+            wide[rest_pair + pair, pl.ds(pl.multiple_of(128 * i + 16, 16), 128)] = block[
+                :, pair * 128 : (pair + 1) * 128
+            ]
+
+    loop(0, 8, rest_rows)
+    for pair in range(3):
+        wide[rest_pair + pair, 0:16] = wide[rest_pair + pair, 1024:1040]
+        wide[rest_pair + pair, 1040:1056] = wide[rest_pair + pair, 16:32]
+    loop(1, 8, lambda j: rest_copy(lax.rem(slot + j, 8)).start())
     own_rest = pltpu.make_async_copy(
-        snd.at[slot, pl.ds(rest_pair, 3)], rcv.at[pl.ds(2 + 3 * half, 3), mem],
+        wide.at[pl.ds(rest_pair, 3), own_rows], rcv.at[pl.ds(2 + 3 * half, 3), mem],
         rest_recv.at[slot],
     )
     own_rest.start()
@@ -217,7 +218,7 @@
     def edge_wait(j):
         frm = lax.rem(slot + j, 8)
         remote(
-            snd.at[0, 0], rcv.at[1 + 7 * (frm // 4), lax.rem(frm, 4)], edge_send.at[frm],
+            wide.at[0, 0:160], rcv.at[1 + 7 * (frm // 4), lax.rem(frm, 4)], edge_send.at[frm],
             edge_recv.at[frm], ring, frm,
         ).wait_recv()
 
@@ -309,7 +310,7 @@
     def rest_wait(j):
         frm = lax.rem(slot + j, 8)
         remote(
-            snd.at[0, 0:3], rcv.at[pl.ds(2 + 3 * (frm // 4), 3), lax.rem(frm, 4)],
+            wide.at[0:3, 0:160], rcv.at[pl.ds(2 + 3 * (frm // 4), 3), lax.rem(frm, 4)],
             rest_send.at[frm], rest_recv.at[frm], ring, frm,
         ).wait_recv()
 
@@ -447,7 +448,7 @@
     )
 
 
-def analysis_kernel(anom_ref, cen_ref, avg_ref, wt_ref, out_ref, yh, yl, zh, zl):
+def analysis_kernel(anom_ref, cen_ref, avg_ref, wt_ref, out_ref, yh, yl, zh, zl, fh, fl):
     row = lax.broadcasted_iota(jnp.int32, (256, 256), 0)
     col = lax.broadcasted_iota(jnp.int32, (256, 256), 1)
     diagonal = row == col
@@ -509,14 +510,15 @@
         following = []
         for p in range(4):
             a, b, after = coefs(ends[p], plains[p])
-            y = (yh[p], yl[p])
-            z = (zh[p], zl[p])
-            factor = split(a * identity - b * product(z, y))
-            ny = product(y, factor)
-            nz = product(factor, z)
+            t = product((zh[p], zl[p]), (yh[p], yl[p]))
+            fh[p], fl[p] = split(a * identity - b * t)
+            following.append(after)
+        for p in range(4):
+            factor = (fh[p], fl[p])
+            ny = product((yh[p], yl[p]), factor)
+            nz = product(factor, (zh[p], zl[p]))
             yh[p], yl[p] = split(ny)
             zh[p], zl[p] = split(nz)
-            following.append(after)
         return (k + 1, some_left(following, plains, k + 1), *following)
 
     last_k, _, *ends = lax.while_loop(
@@ -524,10 +526,12 @@
     )
     for p in range(4):
         a, b, _ = coefs(ends[p], plains[p])
-        z = (zh[p], zl[p])
-        factor = split(a * identity - b * product(z, (yh[p], yl[p])))
-        inverse = product(factor, z)
-        weights = (inverse / jnp.sqrt(scales[p])).astype(BF16)
+        fh[p], fl[p] = split(a * identity - b * product((zh[p], zl[p]), (yh[p], yl[p])))
+    for p in range(4):
+        _, _, after = coefs(ends[p], plains[p])
+        inverse = product((fh[p], fl[p]), (zh[p], zl[p]))
+        middle = jnp.where(plains[p], 1.0, 0.5 + 0.5 * after)
+        weights = (inverse / (middle * jnp.sqrt(scales[p]))).astype(BF16)
         a = anom_ref[p].reshape(512, 256)
         update = jnp.dot(a, weights, preferred_element_type=F32)
         centre = cen_ref[p].reshape(512, 128)
@@ -553,6 +557,7 @@
     from_right,
     snd,
     rcv,
+    pick,
     edge_send,
     edge_recv,
     main_send,
@@ -588,6 +593,46 @@
     ]
     for copy in edges:
         copy.start()
+    sx = wt_ref[4][None]
+    sy = wt_ref[5][None]
+
+    def step_pair(h, pair, y0, y1):
+        x = 8 * h + 2 * pair + 1
+        rows = slice(8 * y0, 8 * y1)
+        low = lax.broadcasted_iota(jnp.int32, (8 * (y1 - y0), 128), 1) < 64
+        here, behind, ahead = slice(y0 + 1, y1 + 1), slice(y0, y1), slice(y0 + 2, y1 + 2)
+        for mh in range(2):
+            even, odd = [
+                stencil(
+                    g[mh, x + k, here], g[mh, x + k - 1, here], g[mh, x + k + 1, here],
+                    g[mh, x + k, behind], g[mh, x + k, ahead], coef_ref[x + k - 1, y0:y1], sx, sy,
+                ).reshape(8 * (y1 - y0), 128)
+                for k in range(2)
+            ]
+            to = 4 * h + 2 * mh
+            snd[to, pair, rows] = jnp.where(low, even, pltpu.roll(odd, 64, 1)).astype(BF16)
+            snd[to + 1, pair, rows] = jnp.where(low, pltpu.roll(even, 64, 1), odd).astype(BF16)
+
+    def parts(half_of):
+        inner = pl.ds(1 - half_of, 3)
+        return [
+            (inner, slice(16, 112)), (3 * half_of, slice(0, 128)), (inner, slice(0, 16)),
+            (inner, slice(112, 128)),
+        ]
+
+    def main_copy(part, to):
+        pairs, rows = parts(to // 4)[part]
+        return remote(
+            snd.at[to, pairs, rows], rcv.at[slot, pairs, rows], main_send.at[part, to],
+            main_recv.at[part, slot], ring, to,
+        )
+
+    def send(part):
+        loop(1, 8, lambda j: main_copy(part, lax.rem(slot + j, 8)).start())
+
+    for h in range(2):
+        loop(1 - h, 4 - h, lambda pair, h=h: step_pair(h, pair, 2, 14))
+    send(0)
     for copy in edges:
         copy.wait()
     for mh in range(2):
@@ -596,67 +641,48 @@
         g[mh, 17, 1:17] = from_below[:, lanes].astype(F32).reshape(16, 8, 128)
         g[mh, 1:17, 0] = from_left[:, lanes].astype(F32).reshape(16, 8, 128)
         g[mh, 1:17, 17] = from_right[:, lanes].astype(F32).reshape(16, 8, 128)
-    sx = wt_ref[4][None]
-    sy = wt_ref[5][None]
-    low = lax.broadcasted_iota(jnp.int32, (128, 128), 1) < 64
-
-    def main_copy(pair, to):
-        return remote(
-            snd.at[pair, to], rcv.at[pair, slot], main_send.at[pair, to],
-            main_recv.at[pair, slot], ring, to,
-        )
-
-    def own_copy(pair):
-        return pltpu.make_async_copy(snd.at[pair, slot], rcv.at[pair, slot], own_sem.at[pair])
-
-    def send_pair(pair):
+    for h in range(2):
+        step_pair(h, 3 * h, 0, 16)
+    send(1)
+    for y0 in (0, 14):
         for h in range(2):
-            x = 8 * h + 2 * pair + 1
-            for mh in range(2):
-                even, odd = [
-                    stencil(
-                        g[mh, x + k, 1:17], g[mh, x + k - 1, 1:17], g[mh, x + k + 1, 1:17],
-                        g[mh, x + k, 0:16], g[mh, x + k, 2:18], coef_ref[x + k - 1], sx, sy,
-                    ).reshape(128, 128)
-                    for k in range(2)
-                ]
-                snd[pair, 4 * h + 2 * mh] = jnp.where(low, even, pltpu.roll(odd, 64, 1)).astype(BF16)
-                snd[pair, 4 * h + 2 * mh + 1] = jnp.where(low, pltpu.roll(even, 64, 1), odd).astype(BF16)
-        loop(1, 8, lambda j: main_copy(pair, lax.rem(slot + j, 8)).start())
-        own_copy(pair).start()
-
-    loop(0, 4, send_pair)
-
-    row = lax.broadcasted_iota(jnp.int32, (1024, 128), 0)
-    lane = lax.broadcasted_iota(jnp.int32, (1024, 128), 1)
-    same = row // 8 == lane
-    level = lax.rem(row, 8)
-    pick = jnp.concatenate(
-        [jnp.where(same & (level == f), 1.0, 0.0).astype(BF16) for f in range(8)], axis=1
-    )
-
-    def receive_pair(pair):
-        own_copy(pair).wait()
-
-        def wait(j):
+            loop(1 - h, 4 - h, lambda pair, h=h, y0=y0: step_pair(h, pair, y0, y0 + 2))
+    send(2)
+    send(3)
+    own = pltpu.make_async_copy(snd.at[slot], rcv.at[slot], own_sem)
+    own.start()
+
+    def pick_rows(i):
+        row = lax.broadcasted_iota(jnp.int32, (128, 128), 0) + 128 * i
+        lane = lax.broadcasted_iota(jnp.int32, (128, 128), 1)
+        level = jnp.where(row // 8 == lane, lax.rem(row, 8), 8)
+        rows = pl.ds(pl.multiple_of(128 * i, 128), 128)
+        for f in range(8):
+            pick[rows, f * 128 : f * 128 + 128] = jnp.where(level == f, 1.0, 0.0).astype(BF16)
+
+    loop(0, 8, pick_rows)
+    own.wait()
+    for part in range(4):
+
+        def wait(j, part=part):
             frm = lax.rem(slot + j, 8)
+            pairs, rows = parts(half)[part]
             remote(
-                snd.at[pair, frm], rcv.at[pair, frm], main_send.at[pair, frm],
-                main_recv.at[pair, frm], ring, frm,
+                snd.at[frm, pairs, rows], rcv.at[frm, pairs, rows], main_send.at[part, frm],
+                main_recv.at[part, frm], ring, frm,
             ).wait_recv()
 
         loop(1, 8, wait)
-        block = rcv[pair].reshape(1024, 128)
-        result = lax.dot_general(block, pick, TN, preferred_element_type=F32).astype(BF16)
+
+    def result_pair(pair):
+        block = rcv[:, pair].reshape(1024, 128)
+        result = lax.dot_general(block, pick[...], TN, preferred_element_type=F32).astype(BF16)
         out_ref[2 * pair] = result[:64]
         out_ref[2 * pair + 1] = result[64:]
 
-    loop(0, 4, receive_pair)
-
-    def finish(pair):
-        loop(1, 8, lambda j: main_copy(pair, lax.rem(slot + j, 8)).wait_send())
-
-    loop(0, 4, finish)
+    loop(0, 4, result_pair)
+    for part in range(4):
+        loop(1, 8, lambda j, part=part: main_copy(part, lax.rem(slot + j, 8)).wait_send())
 
 
 def vmem(count):
@@ -689,8 +715,9 @@
             pltpu.SMEM((8,), F32),
             pltpu.VMEM((1, 256), jnp.int32),
             pltpu.VMEM((512, 1024), BF16),
-            pltpu.VMEM((8, 160, 1024), BF16),
-            pltpu.VMEM((8, 4, 160, 128), BF16),
+            pltpu.VMEM((512, 1024), BF16),
+            pltpu.VMEM((1024, 1024), BF16),
+            pltpu.VMEM((4, 1056, 128), BF16),
             pltpu.VMEM((10, 4, 160, 128), BF16),
             pltpu.VMEM((2, 20, 20, 8, 128), F32),
             pltpu.VMEM((2, 18, 18, 8, 128), F32),
@@ -730,7 +757,7 @@
         out_shape=shape((16, 128, 256), BF16),
         in_specs=vmem(4),
         out_specs=pl.BlockSpec(memory_space=pltpu.VMEM),
-        scratch_shapes=[pltpu.VMEM((4, 256, 256), BF16)] * 4,
+        scratch_shapes=[pltpu.VMEM((4, 256, 256), BF16)] * 6,
         compiler_params=pltpu.CompilerParams(vmem_limit_bytes=VMEM_LIMIT),
     )(anom, cen, avg, wt)
 
@@ -747,13 +774,14 @@
             pltpu.VMEM((128, 256), BF16),
             pltpu.VMEM((128, 256), BF16),
             pltpu.VMEM((128, 256), BF16),
-            pltpu.VMEM((4, 8, 128, 128), BF16),
-            pltpu.VMEM((4, 8, 128, 128), BF16),
+            pltpu.VMEM((8, 4, 128, 128), BF16),
+            pltpu.VMEM((8, 4, 128, 128), BF16),
+            pltpu.VMEM((1024, 1024), BF16),
             DMA((4,)),
             DMA((4,)),
             DMA((4, 8)),
             DMA((4, 8)),
-            DMA((4,)),
+            DMA,
         ],
         compiler_params=pltpu.CompilerParams(
             collective_id=1, has_side_effects=True, vmem_limit_bytes=VMEM_LIMIT

time: 79.7 us -> 75.5 us (0.947)
  Pallas kernels: 74.9 us -> 70.7 us
    pallas_call x1, Pallas kernels: 8.26 us -> 5.04 us  [local(): pl.pallas_call(analysis_kernel, out_shape=shape((16, 128, 256), BF16), in...]
    pallas_call x1, Pallas kernels: 23.9 us -> 21.8 us  [local(): pl.pallas_call(lambda *refs: return_kernel(rings, *refs), out_shape=shape...]
    pallas_call x1, Pallas kernels: 42.7 us -> 43.9 us  [local(): pl.pallas_call(lambda *refs: forecast_kernel(rings, *refs), out_shape=[sh...]
where the time goes in v2:
time: 75.5 us; the launch traced here: 75.3 us
  Pallas kernels  70.7 us (94%)
  local copies, waits for them, and re-layouts  4.55 us (6%)
    pallas_call x1, Pallas kernels, local(): pl.pallas_call(lambda *refs: forecast_kernel(rings, *refs), out_shape=[sh...  43.9 us
    pallas_call x1, Pallas kernels, local(): pl.pallas_call(lambda *refs: return_kernel(rings, *refs), out_shape=shape...  21.8 us
    pallas_call x1, Pallas kernels, local(): pl.pallas_call(analysis_kernel, out_shape=shape((16, 128, 256), BF16), in...  5.04 us
    unnamed x9, local copies, waits for them, and re-layouts  2.36 us
    reshape x1, local copies, waits for them, and re-layouts, local(): return jnp.transpose(out.reshape(8, 64, 8, 128), (1, 2, 0, 3))  2.2 us

profile of v2, /device:TPU:1, one launch (start us, length us, event | category | flops | bytes accessed | tf_op | source)
XLA Modules:
  0.0 75.3 jit_solution(3213923845893662014)
XLA Ops:
  0.0 0.0 copy-start.1
  0.0 0.0 copy-start.2
  0.0 0.7 copy-done.1
  0.7 0.0 copy-done.2
  0.7 0.0 copy-start
  0.7 0.8 %copy-done = f32[8,8,128]{2,1,0:T(8,128)S(1)} copy-done((f32[8,8,128]{2,1,0:T(8,128)S(1)}, f32[8,8,128]{2,1,0:T(8,128)}, u32[]{:S(2)}) %copy-start) | copy-done | bytes 32792
  1.4 0.0 copy-start.3
  1.4 0.7 copy-done.3
  2.1 43.9 %shard_map.55 = (bf16[4,8,64,256]{3,2,1,0:T(8,128)(2,1)S(1)}, f32[4,8,64,128]{3,2,1,0:T(8,128)S(1)}, f32[4,264,128]{2,1,0:T(8,128)S(1)}, f32[6,8,128]{2,1,0:T(8,128)S(1)}, f32[16,16,8,128]{3,2,1,0:T(8,128)S(1)}) custom-call(bf16[64,8,8,128]{3,2,1,0:T(8,128)(2,1)} %refs_0_.1, f32[8,8,128]{2,1,0:T(8,128)S(1)} %copy-done, f32[8]{0:T(128)S(1)} %copy-done.2, ...), custom_call_target="tpu_custom_call" | custom-call | tf_op jit(solution)/shard_map/pallas_call | solution.py:700
  46.0 5.0 %shard_map.56.refs_0_ = bf16[16,128,256]{2,1,0:T(8,128)(2,1)S(1)} custom-call(bf16[4,8,64,256]{3,2,1,0:T(8,128)(2,1)S(1)} %get-tuple-element.10.anom_ref, f32[4,8,64,128]{3,2,1,0:T(8,128)S(1)} %get-tuple-element.11.cen_ref, f32[4,264,128]{2,1,0:T(8,128)S(1)} %get-tuple-element.12.avg_ref, f32[6,8,128]{2,1,0:T(8,128)S(1)} %get-tuple-element.13.wt_ref.refs_2_), custom_call_target="tpu_custom_call" | custom-call | tf_op jit(solution)/shard_map/pallas_call | solution.py:755
  51.0 21.8 %shard_map.57 = bf16[8,64,1024]{2,1,0:T(8,128)(2,1)S(1)} custom-call(bf16[16,128,256]{2,1,0:T(8,128)(2,1)S(1)} %shard_map.56.refs_0_, f32[16,16,8,128]{3,2,1,0:T(8,128)S(1)} %get-tuple-element.14.refs_1_, f32[6,8,128]{2,1,0:T(8,128)S(1)} %get-tuple-element.13.wt_ref.refs_2_), custom_call_target="tpu_custom_call" | custom-call | tf_op jit(solution)/shard_map/pallas_call | solution.py:764
  72.8 0.3 copy.7
  73.1 2.2 %copy.9 = bf16[8,64,8,128]{3,0,2,1:T(8,128)(2,1)} copy(bf16[8,64,8,128]{3,2,1,0:T(8,128)(2,1)S(1)} %bitcast.10) | data formatting | bytes 2097152 | tf_op jit(solution)/shard_map/reshape | solution.py:790
Async XLA Ops:
  0.0 0.7 copy-start.1
  0.0 0.7 copy-start.2
  0.7 0.8 %copy-start = (f32[8,8,128]{2,1,0:T(8,128)S(1)}, f32[8,8,128]{2,1,0:T(8,128)}, u32[]{:S(2)}) copy-start(f32[8,8,128]{2,1,0:T(8,128)} %refs_1_.1) | copy-start | bytes 98308
  1.4 0.7 copy-start.3

commit v3 on v2

--- a/solution.py
+++ b/solution.py
@@ -63,9 +63,9 @@
     rings,
     u_hbm,
     spread_hbm,
-    sx_hbm,
-    sy_hbm,
     obs_hbm,
+    sx_ref,
+    sy_ref,
     anom_ref,
     cen_ref,
     avg_ref,
@@ -73,8 +73,6 @@
     coef_ref,
     raw,
     spread_in,
-    sx_in,
-    sy_in,
     obs_in,
     flat,
     state,
@@ -94,10 +92,8 @@
     gle,
     gri,
     load_sem,
-    edge_send,
-    edge_recv,
-    rest_send,
-    rest_recv,
+    block_send,
+    block_recv,
     halo_send,
     halo_recv,
     spr_send,
@@ -116,17 +112,12 @@
     barrier = pltpu.get_barrier_semaphore()
     loop(1, 8, lambda j: signal(barrier, ring, lax.rem(slot + j, 8)))
     loop(1, rings, lambda j: signal(barrier, lax.rem(ring + j, rings), slot))
-    loads = [
-        pltpu.make_async_copy(src, dst, load_sem.at[k])
-        for k, (src, dst) in enumerate(
-            [
-                (u_hbm, raw), (spread_hbm, spread_in), (sx_hbm, sx_in), (sy_hbm, sy_in),
-                (obs_hbm, obs_in),
-            ]
-        )
-    ]
-    for copy in loads:
-        copy.start()
+    load_raw = pltpu.make_async_copy(u_hbm, raw, load_sem.at[0])
+    load_spread = pltpu.make_async_copy(spread_hbm, spread_in, load_sem.at[1])
+    load_obs = pltpu.make_async_copy(obs_hbm, obs_in, load_sem.at[2])
+    load_raw.start()
+    load_spread.start()
+    load_obs.start()
 
     def pick_rows(i):
         row = lax.broadcasted_iota(jnp.int32, (128, 128), 0) + 128 * i
@@ -138,72 +129,68 @@
 
     loop(0, 8, pick_rows)
 
-    edge_pair = 3 * half
-    rest_pair = 1 - half
-
-    def turned(first, count):
-        k = lax.broadcasted_iota(jnp.int32, (128 * count, 512), 1)
-        r = lax.broadcasted_iota(jnp.int32, (128 * count, 512), 0) + 128 * first
+    load_raw.wait()
+    for f in range(8):
+        flat[:, f * 128 : f * 128 + 128] = raw[:, f].astype(F32).reshape(512, 128).astype(BF16)
+
+    def pair_of(t, side):
+        return t + side * (3 - 2 * t)
+
+    def place_of(t, side):
+        return 1 + 4 * side + pair_of(t, side)
+
+    def turn_pair(t):
+        pair = pair_of(t, half)
+        k = lax.broadcasted_iota(jnp.int32, (128, 512), 1)
+        r = lax.broadcasted_iota(jnp.int32, (128, 512), 0) + 128 * pair
         turn = jnp.where(k == lax.rem(r, 64) * 8 + r // 64, 1.0, 0.0).astype(BF16)
-        return jnp.dot(turn, flat[...], preferred_element_type=F32).astype(BF16)
-
-    def store_pair(pair, block):
+        state[...] = jnp.dot(turn, flat[...], preferred_element_type=F32).astype(BF16)
+        block = lax.dot_general(
+            pick[...], state[...], NT, preferred_element_type=F32
+        ).astype(BF16)
         wide[pair, 16:1040] = block
         wide[pair, 0:16] = block[1008:1024]
         wide[pair, 1040:1056] = block[0:16]
 
-    loads[0].wait()
-    for f in range(8):
-        flat[:, f * 128 : f * 128 + 128] = raw[:, f].astype(F32).reshape(512, 128).astype(BF16)
-    state[0:128] = turned(edge_pair, 1)
-    store_pair(
-        edge_pair,
-        lax.dot_general(pick[...], state[0:128], NT, preferred_element_type=F32).astype(BF16),
-    )
-
-    def edge_copy(to):
+    def block_copy(t, to):
         return remote(
-            wide.at[edge_pair, pl.ds(pl.multiple_of(128 * to, 128), 160)],
-            rcv.at[1 + 7 * half, mem], edge_send.at[to], edge_recv.at[slot], ring, to,
+            wide.at[pair_of(t, half), pl.ds(pl.multiple_of(128 * to, 128), 160)],
+            rcv.at[place_of(t, half), mem], block_send.at[t, to], block_recv.at[t, slot], ring, to,
         )
 
-    def rest_copy(to):
-        return remote(
-            wide.at[pl.ds(rest_pair, 3), pl.ds(pl.multiple_of(128 * to, 128), 160)],
-            rcv.at[pl.ds(2 + 3 * half, 3), mem], rest_send.at[to], rest_recv.at[slot], ring, to,
+    def own_copy(t):
+        return pltpu.make_async_copy(
+            wide.at[pair_of(t, half), pl.ds(pl.multiple_of(128 * slot, 128), 160)],
+            rcv.at[place_of(t, half), mem], block_recv.at[t, slot],
         )
 
+    def send_blocks(t):
+        loop(1, 8, lambda j: block_copy(t, lax.rem(slot + j, 8)).start())
+        own_copy(t).start()
+
+    def wait_blocks(t):
+        own_copy(t).wait()
+
+        def wait(j):
+            frm = lax.rem(slot + j, 8)
+            remote(
+                wide.at[0, 0:160], rcv.at[place_of(t, frm // 4), lax.rem(frm, 4)],
+                block_send.at[t, frm], block_recv.at[t, frm], ring, frm,
+            ).wait_recv()
+
+        loop(1, 8, wait)
+
+    turn_pair(0)
     pl.semaphore_wait(barrier, 7 + rings - 1)
-    loop(1, 8, lambda j: edge_copy(lax.rem(slot + j, 8)).start())
-    own_rows = pl.ds(pl.multiple_of(128 * slot, 128), 160)
-    own_edge = pltpu.make_async_copy(
-        wide.at[edge_pair, own_rows], rcv.at[1 + 7 * half, mem], edge_recv.at[slot]
-    )
-    own_edge.start()
-    state[128:512] = turned(rest_pair, 3)
-
-    def rest_rows(i):
-        rows = pl.ds(pl.multiple_of(128 * i, 128), 128)
-        block = lax.dot_general(
-            pick[rows, :], state[128:512], NT, preferred_element_type=F32
-        ).astype(BF16)
-        for pair in range(3):
-            wide[rest_pair + pair, pl.ds(pl.multiple_of(128 * i + 16, 16), 128)] = block[
-                :, pair * 128 : (pair + 1) * 128
-            ]
-
-    loop(0, 8, rest_rows)
-    for pair in range(3):
-        wide[rest_pair + pair, 0:16] = wide[rest_pair + pair, 1024:1040]
-        wide[rest_pair + pair, 1040:1056] = wide[rest_pair + pair, 16:32]
-    loop(1, 8, lambda j: rest_copy(lax.rem(slot + j, 8)).start())
-    own_rest = pltpu.make_async_copy(
-        wide.at[pl.ds(rest_pair, 3), own_rows], rcv.at[pl.ds(2 + 3 * half, 3), mem],
-        rest_recv.at[slot],
-    )
-    own_rest.start()
-
-    loads[1].wait()
+    send_blocks(0)
+
+    def next_pair(t):
+        turn_pair(t)
+        send_blocks(t)
+
+    loop(1, 4, next_pair)
+
+    load_spread.wait()
     mine = 8 + 8 * half
     for x in range(8):
         spr[mine + x] = spread_in[:, x, :]
@@ -213,16 +200,7 @@
     )
     spr_here.start()
 
-    own_edge.wait()
-
-    def edge_wait(j):
-        frm = lax.rem(slot + j, 8)
-        remote(
-            wide.at[0, 0:160], rcv.at[1 + 7 * (frm // 4), lax.rem(frm, 4)], edge_send.at[frm],
-            edge_recv.at[frm], ring, frm,
-        ).wait_recv()
-
-    loop(1, 8, edge_wait)
+    wait_blocks(0)
     halos = [
         remote(rcv.at[1], rcv.at[9], halo_send.at[0], halo_recv.at[0], above, slot),
         remote(rcv.at[8], rcv.at[0], halo_send.at[1], halo_recv.at[1], below, slot),
@@ -230,7 +208,7 @@
     for copy in halos:
         copy.start()
 
-    loads[4].wait()
+    load_obs.wait()
     obs = obs_in[...]
     in_ring = lax.broadcasted_iota(jnp.int32, (rings, 256), 0) == obs // 32
     in_patch = lax.broadcasted_iota(jnp.int32, (128, 256), 0) == lax.rem(obs, 32)
@@ -279,10 +257,8 @@
         copy.wait()
     for i in (0, 1, 18, 19):
         spread_row(i)
-    loads[2].wait()
-    loads[3].wait()
     sublane = lax.broadcasted_iota(jnp.int32, (8, 128), 0)
-    for k, ref in enumerate((sx_in, sy_in)):
+    for k, ref in enumerate((sx_ref, sy_ref)):
         speed = jnp.zeros((8, 128), F32)
         for f in range(8):
             speed = jnp.where(sublane == f, ref[f], speed)
@@ -305,17 +281,6 @@
     unshuffle(0)
     unshuffle(9)
 
-    own_rest.wait()
-
-    def rest_wait(j):
-        frm = lax.rem(slot + j, 8)
-        remote(
-            wide.at[0:3, 0:160], rcv.at[pl.ds(2 + 3 * (frm // 4), 3), lax.rem(frm, 4)],
-            rest_send.at[frm], rest_recv.at[frm], ring, frm,
-        ).wait_recv()
-
-    loop(1, 8, rest_wait)
-    loop(2, 8, unshuffle)
     sx = wt_ref[4][None]
     sy = wt_ref[5][None]
 
@@ -329,7 +294,49 @@
                 )
             )
 
-    loop(1, 19, first)
+    def second(row, c):
+        h, i = row // 8, lax.rem(row, 8)
+        x, y = row + 1, 8 * c + 1
+        s = coef[x + 1, y + 1 : y + 9]
+        prior = [
+            rounded(
+                stencil(
+                    u1[mh, x, y : y + 8], u1[mh, x - 1, y : y + 8], u1[mh, x + 1, y : y + 8],
+                    u1[mh, x, y - 1 : y + 7], u1[mh, x, y + 1 : y + 9], s, sx, sy,
+                )
+            )
+            for mh in range(2)
+        ]
+        centre = jnp.sum(prior[0] + prior[1], axis=2, keepdims=True) * (1.0 / 256.0)
+        centre = jnp.broadcast_to(centre, (8, 8, 128))
+        cen_ref[2 * h + c, i] = centre.reshape(64, 128)
+        for mh in range(2):
+            anom_ref[2 * h + c, i, :, mh * 128 : mh * 128 + 128] = (
+                (prior[mh] - centre).reshape(64, 128).astype(BF16)
+            )
+
+    loop(1, 3, first)
+    loop(17, 19, first)
+
+    def inwards(t):
+        wait_blocks(t)
+        unshuffle(1 + t)
+        unshuffle(8 - t)
+
+        def firsts(k):
+            first(2 * t + 1 + k)
+            first(17 - 2 * t + k)
+
+        loop(0, 2, firsts)
+
+        def seconds(k):
+            for c in range(2):
+                second(2 * t - 2 + k, c)
+                second(16 - 2 * t + k, c)
+
+        loop(0, 2, seconds)
+
+    loop(1, 3, inwards)
 
     def count_wait(j):
         frm = lax.rem(ring + j, rings)
@@ -348,6 +355,11 @@
         )
 
     loop(1, 8, lambda j: sum_copy(j).start())
+
+    wait_blocks(3)
+    unshuffle(4)
+    unshuffle(5)
+    loop(7, 13, first)
 
     row = lax.broadcasted_iota(jnp.int32, (128, 128), 0)
     col = lax.broadcasted_iota(jnp.int32, (128, 128), 1)
@@ -358,29 +370,7 @@
         for h in range(2):
             p = 2 * h + c
 
-            def second(i, h=h, c=c, p=p):
-                x = 8 * h + i + 1
-                y = 8 * c + 1
-                s = coef[x + 1, y + 1 : y + 9]
-                prior = [
-                    rounded(
-                        stencil(
-                            u1[mh, x, y : y + 8], u1[mh, x - 1, y : y + 8],
-                            u1[mh, x + 1, y : y + 8], u1[mh, x, y - 1 : y + 7],
-                            u1[mh, x, y + 1 : y + 9], s, sx, sy,
-                        )
-                    )
-                    for mh in range(2)
-                ]
-                centre = jnp.sum(prior[0] + prior[1], axis=2, keepdims=True) * (1.0 / 256.0)
-                centre = jnp.broadcast_to(centre, (8, 8, 128))
-                cen_ref[p, i] = centre.reshape(64, 128)
-                for mh in range(2):
-                    anom_ref[p, i, :, mh * 128 : mh * 128 + 128] = (
-                        (prior[mh] - centre).reshape(64, 128).astype(BF16)
-                    )
-
-            loop(0, 8, second)
+            loop(4 + 4 * h, 8 + 4 * h, lambda row, c=c: second(row, c))
             a = anom_ref[p].reshape(512, 256)
             g = lax.dot_general(a, a, TN, preferred_element_type=F32) * (1.0 / 512.0)
             last = g[128:, 128:]
@@ -420,8 +410,7 @@
             wt_ref[2 * h + c] = jnp.broadcast_to(count / (count + 16.0), (8, 128))
     loop(1, rings, lambda j: count_copy(j).wait_send())
     loop(1, 8, lambda j: sum_copy(j).wait_send())
-    loop(1, 8, lambda j: edge_copy(lax.rem(slot + j, 8)).wait_send())
-    loop(1, 8, lambda j: rest_copy(lax.rem(slot + j, 8)).wait_send())
+    loop(0, 4, lambda t: loop(1, 8, lambda j: block_copy(t, lax.rem(slot + j, 8)).wait_send()))
     for copy in copies:
         copy.wait()
     for c in range(2):
@@ -448,7 +437,7 @@
     )
 
 
-def analysis_kernel(anom_ref, cen_ref, avg_ref, wt_ref, out_ref, yh, yl, zh, zl, fh, fl):
+def analysis_kernel(avg_ref, wt_ref, yh, yl, zh, zl, last_ref, fh, fl):
     row = lax.broadcasted_iota(jnp.int32, (256, 256), 0)
     col = lax.broadcasted_iota(jnp.int32, (256, 256), 1)
     diagonal = row == col
@@ -525,36 +514,29 @@
         lambda carry: carry[1], body, (1, some_left(ends, plains, 1), *ends)
     )
     for p in range(4):
-        a, b, _ = coefs(ends[p], plains[p])
-        fh[p], fl[p] = split(a * identity - b * product((zh[p], zl[p]), (yh[p], yl[p])))
-    for p in range(4):
-        _, _, after = coefs(ends[p], plains[p])
-        inverse = product((fh[p], fl[p]), (zh[p], zl[p]))
+        a, b, after = coefs(ends[p], plains[p])
         middle = jnp.where(plains[p], 1.0, 0.5 + 0.5 * after)
-        weights = (inverse / (middle * jnp.sqrt(scales[p]))).astype(BF16)
-        a = anom_ref[p].reshape(512, 256)
-        update = jnp.dot(a, weights, preferred_element_type=F32)
-        centre = cen_ref[p].reshape(512, 128)
-        centre = jnp.concatenate([centre, centre], axis=1)
-        h, c = p // 2, p % 2
-        out_ref[8 * h : 8 * h + 8, 64 * c : 64 * c + 64, :] = (
-            (centre + update).astype(BF16).reshape(8, 64, 256)
-        )
+        for k, value in enumerate((a, b, 1.0 / (middle * jnp.sqrt(scales[p])))):
+            last_ref[3 * p + k] = jnp.broadcast_to(value, (8, 128))
 
 
 def return_kernel(
     rings,
-    f_ref,
+    anom_ref,
+    cen_ref,
+    yh,
+    yl,
+    zh,
+    zl,
+    last_ref,
     coef_ref,
     wt_ref,
     out_ref,
+    fh,
+    fl,
     g,
-    west,
-    east,
-    from_above,
-    from_below,
-    from_left,
-    from_right,
+    edge_out,
+    edge_in,
     snd,
     rcv,
     pick,
@@ -574,22 +556,34 @@
     signal(barrier, above, slot)
     signal(barrier, below, slot)
 
-    def widen(x):
-        plane = f_ref[x].astype(F32)
+    diagonal = lax.broadcasted_iota(jnp.int32, (256, 256), 0) == lax.broadcasted_iota(
+        jnp.int32, (256, 256), 1
+    )
+    for p in range(4):
+        t = product((zh[p], zl[p]), (yh[p], yl[p]))
+        a, b = last_ref[3 * p, 0:1, 0:1], last_ref[3 * p + 1, 0:1, 0:1]
+        fh[p], fl[p] = split(jnp.where(diagonal, a, 0.0) - b * t)
+    for p in range(4):
+        inverse = product((fh[p], fl[p]), (zh[p], zl[p]))
+        weights = (inverse * last_ref[3 * p + 2, 0:1, 0:1]).astype(BF16)
+        update = jnp.dot(anom_ref[p].reshape(512, 256), weights, preferred_element_type=F32)
+        centre = cen_ref[p].reshape(512, 128)
+        h, c = p // 2, p % 2
         for mh in range(2):
-            g[mh, x + 1, 1:17] = plane[:, mh * 128 : mh * 128 + 128].reshape(16, 8, 128)
-
-    loop(0, 16, widen)
+            value = rounded(centre + update[:, mh * 128 : mh * 128 + 128])
+            g[mh, 8 * h + 1 : 8 * h + 9, 8 * c + 1 : 8 * c + 9] = value.reshape(8, 8, 8, 128)
     for mh in range(2):
         lanes = slice(mh * 128, mh * 128 + 128)
-        west[:, lanes] = g[mh, 1:17, 1].reshape(128, 128).astype(BF16)
-        east[:, lanes] = g[mh, 1:17, 16].reshape(128, 128).astype(BF16)
+        edge_out[0, :, lanes] = g[mh, 1, 1:17].reshape(128, 128).astype(BF16)
+        edge_out[1, :, lanes] = g[mh, 16, 1:17].reshape(128, 128).astype(BF16)
+        edge_out[2, :, lanes] = g[mh, 1:17, 1].reshape(128, 128).astype(BF16)
+        edge_out[3, :, lanes] = g[mh, 1:17, 16].reshape(128, 128).astype(BF16)
     pl.semaphore_wait(barrier, 9)
     edges = [
-        remote(f_ref.at[0], from_below, edge_send.at[0], edge_recv.at[0], above, slot),
-        remote(f_ref.at[15], from_above, edge_send.at[1], edge_recv.at[1], below, slot),
-        remote(west, from_right, edge_send.at[2], edge_recv.at[2], ring, left),
-        remote(east, from_left, edge_send.at[3], edge_recv.at[3], ring, right),
+        remote(edge_out.at[k], edge_in.at[k], edge_send.at[k], edge_recv.at[k], to_ring, to_slot)
+        for k, (to_ring, to_slot) in enumerate(
+            [(above, slot), (below, slot), (ring, left), (ring, right)]
+        )
     ]
     for copy in edges:
         copy.start()
@@ -616,8 +610,8 @@
     def parts(half_of):
         inner = pl.ds(1 - half_of, 3)
         return [
-            (inner, slice(16, 112)), (3 * half_of, slice(0, 128)), (inner, slice(0, 16)),
-            (inner, slice(112, 128)),
+            (inner, slice(16, 112)), (inner, slice(0, 16)), (inner, slice(112, 128)),
+            (3 * half_of, slice(0, 128)),
         ]
 
     def main_copy(part, to):
@@ -637,17 +631,16 @@
         copy.wait()
     for mh in range(2):
         lanes = slice(mh * 128, mh * 128 + 128)
-        g[mh, 0, 1:17] = from_above[:, lanes].astype(F32).reshape(16, 8, 128)
-        g[mh, 17, 1:17] = from_below[:, lanes].astype(F32).reshape(16, 8, 128)
-        g[mh, 1:17, 0] = from_left[:, lanes].astype(F32).reshape(16, 8, 128)
-        g[mh, 1:17, 17] = from_right[:, lanes].astype(F32).reshape(16, 8, 128)
+        g[mh, 17, 1:17] = edge_in[0, :, lanes].astype(F32).reshape(16, 8, 128)
+        g[mh, 0, 1:17] = edge_in[1, :, lanes].astype(F32).reshape(16, 8, 128)
+        g[mh, 1:17, 17] = edge_in[2, :, lanes].astype(F32).reshape(16, 8, 128)
+        g[mh, 1:17, 0] = edge_in[3, :, lanes].astype(F32).reshape(16, 8, 128)
+    for part, y0 in ((1, 0), (2, 14)):
+        for h in range(2):
+            loop(1 - h, 4 - h, lambda pair, h=h, y0=y0: step_pair(h, pair, y0, y0 + 2))
+        send(part)
     for h in range(2):
         step_pair(h, 3 * h, 0, 16)
-    send(1)
-    for y0 in (0, 14):
-        for h in range(2):
-            loop(1 - h, 4 - h, lambda pair, h=h, y0=y0: step_pair(h, pair, y0, y0 + 2))
-    send(2)
     send(3)
     own = pltpu.make_async_copy(snd.at[slot], rcv.at[slot], own_sem)
     own.start()
@@ -662,9 +655,9 @@
 
     loop(0, 8, pick_rows)
     own.wait()
-    for part in range(4):
-
-        def wait(j, part=part):
+
+    def wait_part(part):
+        def wait(j):
             frm = lax.rem(slot + j, 8)
             pairs, rows = parts(half)[part]
             remote(
@@ -680,7 +673,11 @@
         out_ref[2 * pair] = result[:64]
         out_ref[2 * pair + 1] = result[64:]
 
-    loop(0, 4, result_pair)
+    for part in range(3):
+        wait_part(part)
+    loop(1 - half, 4 - half, result_pair)
+    wait_part(3)
+    result_pair(3 * half)
     for part in range(4):
         loop(1, 8, lambda j, part=part: main_copy(part, lax.rem(slot + j, 8)).wait_send())
 
@@ -706,16 +703,15 @@
             shape((6, 8, 128)),
             shape((16, 16, 8, 128)),
         ],
-        in_specs=[pl.BlockSpec(memory_space=pltpu.HBM)] * 5,
+        in_specs=[pl.BlockSpec(memory_space=pltpu.HBM)] * 3
+        + [pl.BlockSpec(memory_space=pltpu.SMEM)] * 2,
         out_specs=vmem(5),
         scratch_shapes=[
             pltpu.VMEM((64, 8, 8, 128), BF16),
             pltpu.VMEM((8, 8, 128), F32),
-            pltpu.SMEM((8,), F32),
-            pltpu.SMEM((8,), F32),
             pltpu.VMEM((1, 256), jnp.int32),
             pltpu.VMEM((512, 1024), BF16),
-            pltpu.VMEM((512, 1024), BF16),
+            pltpu.VMEM((128, 1024), BF16),
             pltpu.VMEM((1024, 1024), BF16),
             pltpu.VMEM((4, 1056, 128), BF16),
             pltpu.VMEM((10, 4, 160, 128), BF16),
@@ -731,11 +727,9 @@
             pltpu.VMEM((2, 264, 128), F32),
             pltpu.VMEM((2, 264, 128), F32),
             pltpu.VMEM((2, 264, 128), F32),
-            DMA((5,)),
-            DMA((8,)),
-            DMA((8,)),
-            DMA((8,)),
-            DMA((8,)),
+            DMA((3,)),
+            DMA((4, 8)),
+            DMA((4, 8)),
             DMA((2,)),
             DMA((2,)),
             DMA((3,)),
@@ -750,30 +744,29 @@
         compiler_params=pltpu.CompilerParams(
             collective_id=0, has_side_effects=True, vmem_limit_bytes=VMEM_LIMIT
         ),
-    )(member_collection, spreading_ratio, transport_ratio_row, transport_ratio_column, obs)
-
-    field = pl.pallas_call(
+    )(member_collection, spreading_ratio, obs, transport_ratio_row, transport_ratio_column)
+
+    square = shape((4, 256, 256), BF16)
+    yh, yl, zh, zl, last = pl.pallas_call(
         analysis_kernel,
-        out_shape=shape((16, 128, 256), BF16),
-        in_specs=vmem(4),
-        out_specs=pl.BlockSpec(memory_space=pltpu.VMEM),
-        scratch_shapes=[pltpu.VMEM((4, 256, 256), BF16)] * 6,
-        compiler_params=pltpu.CompilerParams(vmem_limit_bytes=VMEM_LIMIT),
-    )(anom, cen, avg, wt)
+        out_shape=[square, square, square, square, shape((12, 8, 128))],
+        in_specs=vmem(2),
+        out_specs=vmem(5),
+        scratch_shapes=[pltpu.VMEM((4, 256, 256), BF16)] * 2,
+        compiler_params=pltpu.CompilerParams(vmem_limit_bytes=16 * 1024 * 1024),
+    )(avg, wt)
 
     out = pl.pallas_call(
         lambda *refs: return_kernel(rings, *refs),
         out_shape=shape((8, 64, 1024), BF16),
-        in_specs=vmem(3),
+        in_specs=vmem(9),
         out_specs=pl.BlockSpec(memory_space=pltpu.VMEM),
         scratch_shapes=[
+            pltpu.VMEM((4, 256, 256), BF16),
+            pltpu.VMEM((4, 256, 256), BF16),
             pltpu.VMEM((2, 18, 18, 8, 128), F32),
-            pltpu.VMEM((128, 256), BF16),
-            pltpu.VMEM((128, 256), BF16),
-            pltpu.VMEM((128, 256), BF16),
-            pltpu.VMEM((128, 256), BF16),
-            pltpu.VMEM((128, 256), BF16),
-            pltpu.VMEM((128, 256), BF16),
+            pltpu.VMEM((4, 128, 256), BF16),
+            pltpu.VMEM((4, 128, 256), BF16),
             pltpu.VMEM((8, 4, 128, 128), BF16),
             pltpu.VMEM((8, 4, 128, 128), BF16),
             pltpu.VMEM((1024, 1024), BF16),
@@ -784,9 +777,9 @@
             DMA,
         ],
         compiler_params=pltpu.CompilerParams(
-            collective_id=1, has_side_effects=True, vmem_limit_bytes=VMEM_LIMIT
+            collective_id=1, has_side_effects=True, vmem_limit_bytes=24 * 1024 * 1024
         ),
-    )(field, coef, wt)
+    )(anom, cen, yh, yl, zh, zl, last, coef, wt)
     return jnp.transpose(out.reshape(8, 64, 8, 128), (1, 2, 0, 3))
 
 

time: 75.5 us -> 72.8 us (0.964)
  Pallas kernels: 70.7 us -> 67.9 us
    pallas_call x1, Pallas kernels: 21.8 us -> 20.6 us  [local(): pl.pallas_call(lambda *refs: return_kernel(rings, *refs), out_shape=shape...]
    pallas_call x1, Pallas kernels: 43.9 us -> 42.9 us  [local(): pl.pallas_call(lambda *refs: forecast_kernel(rings, *refs), out_shape=[sh...]
where the time goes in v3:
time: 72.8 us; the launch traced here: 72.5 us
  Pallas kernels  67.9 us (93%)
  local copies, waits for them, and re-layouts  4.55 us (6%)
    pallas_call x1, Pallas kernels, local(): pl.pallas_call(lambda *refs: forecast_kernel(rings, *refs), out_shape=[sh...  42.9 us
    pallas_call x1, Pallas kernels, local(): pl.pallas_call(lambda *refs: return_kernel(rings, *refs), out_shape=shape...  20.6 us
    pallas_call x1, Pallas kernels, local(): pl.pallas_call(analysis_kernel, out_shape=[square, square, square, square...  4.44 us
    unnamed x9, local copies, waits for them, and re-layouts  2.36 us
    reshape x1, local copies, waits for them, and re-layouts, local(): return jnp.transpose(out.reshape(8, 64, 8, 128), (1, 2, 0, 3))  2.2 us

profile of v3, /device:TPU:1, one launch (start us, length us, event | category | flops | bytes accessed | tf_op | source)
XLA Modules:
  0.0 72.5 jit_solution(455716389386112479)
XLA Ops:
  0.0 0.0 copy-start.1
  0.0 0.0 copy-start.2
  0.0 0.7 copy-done.1
  0.7 0.0 copy-done.2
  0.7 0.0 copy-start
  0.7 0.8 %copy-done = f32[8,8,128]{2,1,0:T(8,128)S(1)} copy-done((f32[8,8,128]{2,1,0:T(8,128)S(1)}, f32[8,8,128]{2,1,0:T(8,128)}, u32[]{:S(2)}) %copy-start) | copy-done | bytes 32792
  1.4 0.0 copy-start.3
  1.4 0.7 copy-done.3
  2.1 42.9 %shard_map.55 = (bf16[4,8,64,256]{3,2,1,0:T(8,128)(2,1)S(1)}, f32[4,8,64,128]{3,2,1,0:T(8,128)S(1)}, f32[4,264,128]{2,1,0:T(8,128)S(1)}, f32[6,8,128]{2,1,0:T(8,128)S(1)}, f32[16,16,8,128]{3,2,1,0:T(8,128)S(1)}) custom-call(bf16[64,8,8,128]{3,2,1,0:T(8,128)(2,1)} %refs_0_.1, f32[8,8,128]{2,1,0:T(8,128)S(1)} %copy-done, s32[1,256]{1,0:T(1,128)S(1)} %bitcast.9, ...), custom_call_target="tpu_custom_call" | custom-call | tf_op jit(solution)/shard_map/pallas_call | solution.py:697
  45.0 4.4 %shard_map.56 = (bf16[4,256,256]{2,1,0:T(8,128)(2,1)S(1)}, bf16[4,256,256]{2,1,0:T(8,128)(2,1)S(1)}, bf16[4,256,256]{2,1,0:T(8,128)(2,1)S(1)}, bf16[4,256,256]{2,1,0:T(8,128)(2,1)S(1)}, f32[12,8,128]{2,1,0:T(8,128)S(1)}) custom-call(f32[4,264,128]{2,1,0:T(8,128)S(1)} %get-tuple-element.17.avg_ref, f32[6,8,128]{2,1,0:T(8,128)S(1)} %get-tuple-element.18.wt_ref.refs_8_), custom_call_target="tpu_custom_call" | custom-call | tf_op jit(solution)/shard_map/pallas_call | solution.py:750
  49.4 20.6 %shard_map.57 = bf16[8,64,1024]{2,1,0:T(8,128)(2,1)S(1)} custom-call(bf16[4,8,64,256]{3,2,1,0:T(8,128)(2,1)S(1)} %get-tuple-element.15.refs_0_, f32[4,8,64,128]{3,2,1,0:T(8,128)S(1)} %get-tuple-element.16.refs_1_, bf16[4,256,256]{2,1,0:T(8,128)(2,1)S(1)} %get-tuple-element.19.refs_2_, bf16[4,256,256]{2,1,0:T(8,128)(2,1)S(1)} %get-tuple-element.20.refs_3_, ...), custom_call_target="tpu_custom_call" | custom-call | tf_op jit(solution)/shard_map/pallas_call | solution.py:759
  70.1 0.3 copy.7
  70.3 2.2 %copy.9 = bf16[8,64,8,128]{3,0,2,1:T(8,128)(2,1)} copy(bf16[8,64,8,128]{3,2,1,0:T(8,128)(2,1)S(1)} %bitcast.10) | data formatting | bytes 2097152 | tf_op jit(solution)/shard_map/reshape | solution.py:783
Async XLA Ops:
  0.0 0.7 copy-start.1
  0.0 0.7 copy-start.2
  0.7 0.8 %copy-start = (f32[8,8,128]{2,1,0:T(8,128)S(1)}, f32[8,8,128]{2,1,0:T(8,128)}, u32[]{:S(2)}) copy-start(f32[8,8,128]{2,1,0:T(8,128)} %refs_1_.1) | copy-start | bytes 98308
  1.4 0.7 copy-start.3

commit v4 on v3

--- a/solution.py
+++ b/solution.py
@@ -184,12 +184,6 @@
     pl.semaphore_wait(barrier, 7 + rings - 1)
     send_blocks(0)
 
-    def next_pair(t):
-        turn_pair(t)
-        send_blocks(t)
-
-    loop(1, 4, next_pair)
-
     load_spread.wait()
     mine = 8 + 8 * half
     for x in range(8):
@@ -200,13 +194,9 @@
     )
     spr_here.start()
 
-    wait_blocks(0)
-    halos = [
-        remote(rcv.at[1], rcv.at[9], halo_send.at[0], halo_recv.at[0], above, slot),
-        remote(rcv.at[8], rcv.at[0], halo_send.at[1], halo_recv.at[1], below, slot),
-    ]
-    for copy in halos:
-        copy.start()
+    turn_pair(1)
+    send_blocks(1)
+    turn_pair(2)
 
     load_obs.wait()
     obs = obs_in[...]
@@ -224,6 +214,14 @@
         to = lax.rem(ring + j, rings)
         return remote(cst.at[to], cra.at[ring], cnt_send.at[j], cnt_recv.at[ring], to, slot)
 
+    wait_blocks(0)
+    halos = [
+        remote(rcv.at[1], rcv.at[9], halo_send.at[0], halo_recv.at[0], above, slot),
+        remote(rcv.at[8], rcv.at[0], halo_send.at[1], halo_recv.at[1], below, slot),
+    ]
+    for copy in halos:
+        copy.start()
+    send_blocks(2)
     loop(1, rings, lambda j: count_copy(j).start())
 
     spr_here.wait_send()
@@ -239,6 +237,10 @@
     for copy in spr_far:
         copy.start()
 
+    turn_pair(3)
+    loop(1, 8, lambda j: block_copy(1, lax.rem(slot + j, 8)).wait_send())
+    send_blocks(3)
+
     def spread_row(i):
         lane = lax.broadcasted_iota(jnp.int32, (20, 8, 128), 2)
         column = lax.rem(
@@ -253,10 +255,6 @@
         coef_ref[i] = coef[i + 2, 2:18]
 
     loop(0, 16, coef_row)
-    for copy in spr_far:
-        copy.wait()
-    for i in (0, 1, 18, 19):
-        spread_row(i)
     sublane = lax.broadcasted_iota(jnp.int32, (8, 128), 0)
     for k, ref in enumerate((sx_ref, sy_ref)):
         speed = jnp.zeros((8, 128), F32)
@@ -276,11 +274,6 @@
 
     unshuffle(1)
     unshuffle(8)
-    for copy in halos:
-        copy.wait()
-    unshuffle(0)
-    unshuffle(9)
-
     sx = wt_ref[4][None]
     sy = wt_ref[5][None]
 
@@ -315,28 +308,42 @@
                 (prior[mh] - centre).reshape(64, 128).astype(BF16)
             )
 
-    loop(1, 3, first)
-    loop(17, 19, first)
+    def firsts(low, high):
+        def both(k):
+            first(low + k)
+            first(high + k)
+
+        loop(0, 2, both)
+
+    def seconds(low, high):
+        def both(k):
+            for c in range(2):
+                second(low + k, c)
+                second(high + k, c)
+
+        loop(0, 2, both)
 
     def inwards(t):
         wait_blocks(t)
         unshuffle(1 + t)
         unshuffle(8 - t)
-
-        def firsts(k):
-            first(2 * t + 1 + k)
-            first(17 - 2 * t + k)
-
-        loop(0, 2, firsts)
-
-        def seconds(k):
-            for c in range(2):
-                second(2 * t - 2 + k, c)
-                second(16 - 2 * t + k, c)
-
-        loop(0, 2, seconds)
+        firsts(2 * t + 1, 17 - 2 * t)
 
     loop(1, 3, inwards)
+    for copy in spr_far:
+        copy.wait()
+    for i in (0, 1, 18, 19):
+        spread_row(i)
+    for copy in halos:
+        copy.wait()
+    unshuffle(0)
+    unshuffle(9)
+    firsts(1, 17)
+
+    def outer(t):
+        seconds(2 * t, 14 - 2 * t)
+
+    loop(0, 2, outer)
 
     def count_wait(j):
         frm = lax.rem(ring + j, rings)
@@ -410,7 +417,8 @@
             wt_ref[2 * h + c] = jnp.broadcast_to(count / (count + 16.0), (8, 128))
     loop(1, rings, lambda j: count_copy(j).wait_send())
     loop(1, 8, lambda j: sum_copy(j).wait_send())
-    loop(0, 4, lambda t: loop(1, 8, lambda j: block_copy(t, lax.rem(slot + j, 8)).wait_send()))
+    for t in (0, 2, 3):
+        loop(1, 8, lambda j, t=t: block_copy(t, lax.rem(slot + j, 8)).wait_send())
     for copy in copies:
         copy.wait()
     for c in range(2):

time: 72.8 us -> 67.3 us (0.924)
  Pallas kernels: 67.9 us -> 62.5 us
    pallas_call x1, Pallas kernels: 42.9 us -> 39.6 us  [local(): pl.pallas_call(lambda *refs: forecast_kernel(rings, *refs), out_shape=[sh...]
    pallas_call x1, Pallas kernels: 4.44 us -> 2.94 us  [local(): pl.pallas_call(analysis_kernel, out_shape=[square, square, square, square...]
where the time goes in v4:
time: 67.3 us; the launch traced here: 67.1 us
  Pallas kernels  62.5 us (93%)
  local copies, waits for them, and re-layouts  4.55 us (7%)
    pallas_call x1, Pallas kernels, local(): pl.pallas_call(lambda *refs: forecast_kernel(rings, *refs), out_shape=[sh...  39.6 us
    pallas_call x1, Pallas kernels, local(): pl.pallas_call(lambda *refs: return_kernel(rings, *refs), out_shape=shape...  20 us
    pallas_call x1, Pallas kernels, local(): pl.pallas_call(analysis_kernel, out_shape=[square, square, square, square...  2.94 us
    unnamed x9, local copies, waits for them, and re-layouts  2.36 us
    reshape x1, local copies, waits for them, and re-layouts, local(): return jnp.transpose(out.reshape(8, 64, 8, 128), (1, 2, 0, 3))  2.2 us

profile of v4, /device:TPU:1, one launch (start us, length us, event | category | flops | bytes accessed | tf_op | source)
XLA Modules:
  0.0 67.1 jit_solution(13367228842360245547)
XLA Ops:
  0.0 0.0 copy-start.1
  0.0 0.0 copy-start.2
  0.0 0.7 %copy-done.1 = s32[256]{0:T(256)S(1)} copy-done((s32[256]{0:T(256)S(1)}, s32[256]{0:T(256)}, u32[]{:S(2)}) %copy-start.1) | copy-done | bytes 1048
  0.7 0.0 copy-done.2
  0.7 0.0 copy-start
  0.7 0.8 %copy-done = f32[8,8,128]{2,1,0:T(8,128)S(1)} copy-done((f32[8,8,128]{2,1,0:T(8,128)S(1)}, f32[8,8,128]{2,1,0:T(8,128)}, u32[]{:S(2)}) %copy-start) | copy-done | bytes 32792
  1.4 0.0 copy-start.3
  1.4 0.7 copy-done.3
  2.1 39.6 %shard_map.55 = (bf16[4,8,64,256]{3,2,1,0:T(8,128)(2,1)S(1)}, f32[4,8,64,128]{3,2,1,0:T(8,128)S(1)}, f32[4,264,128]{2,1,0:T(8,128)S(1)}, f32[6,8,128]{2,1,0:T(8,128)S(1)}, f32[16,16,8,128]{3,2,1,0:T(8,128)S(1)}) custom-call(bf16[64,8,8,128]{3,2,1,0:T(8,128)(2,1)} %refs_0_.1, f32[8,8,128]{2,1,0:T(8,128)S(1)} %copy-done, s32[1,256]{1,0:T(1,128)S(1)} %bitcast.9, ...), custom_call_target="tpu_custom_call" | custom-call | tf_op jit(solution)/shard_map/pallas_call | solution.py:705
  41.7 2.9 %shard_map.56 = (bf16[4,256,256]{2,1,0:T(8,128)(2,1)S(1)}, bf16[4,256,256]{2,1,0:T(8,128)(2,1)S(1)}, bf16[4,256,256]{2,1,0:T(8,128)(2,1)S(1)}, bf16[4,256,256]{2,1,0:T(8,128)(2,1)S(1)}, f32[12,8,128]{2,1,0:T(8,128)S(1)}) custom-call(f32[4,264,128]{2,1,0:T(8,128)S(1)} %get-tuple-element.17.avg_ref, f32[6,8,128]{2,1,0:T(8,128)S(1)} %get-tuple-element.18.wt_ref.refs_8_), custom_call_target="tpu_custom_call" | custom-call | tf_op jit(solution)/shard_map/pallas_call | solution.py:758
  44.6 20.0 %shard_map.57 = bf16[8,64,1024]{2,1,0:T(8,128)(2,1)S(1)} custom-call(bf16[4,8,64,256]{3,2,1,0:T(8,128)(2,1)S(1)} %get-tuple-element.15.refs_0_, f32[4,8,64,128]{3,2,1,0:T(8,128)S(1)} %get-tuple-element.16.refs_1_, bf16[4,256,256]{2,1,0:T(8,128)(2,1)S(1)} %get-tuple-element.19.refs_2_, bf16[4,256,256]{2,1,0:T(8,128)(2,1)S(1)} %get-tuple-element.20.refs_3_, ...), custom_call_target="tpu_custom_call" | custom-call | tf_op jit(solution)/shard_map/pallas_call | solution.py:767
  64.6 0.3 copy.7
  64.9 2.2 %copy.9 = bf16[8,64,8,128]{3,0,2,1:T(8,128)(2,1)} copy(bf16[8,64,8,128]{3,2,1,0:T(8,128)(2,1)S(1)} %bitcast.10) | data formatting | bytes 2097152 | tf_op jit(solution)/shard_map/reshape | solution.py:791
Async XLA Ops:
  0.0 0.7 %copy-start.1 = (s32[256]{0:T(256)S(1)}, s32[256]{0:T(256)}, u32[]{:S(2)}) copy-start(s32[256]{0:T(256)} %param.9) | copy-start | bytes 3076
  0.0 0.7 %copy-start.2 = (f32[8]{0:T(128)S(1)}, f32[8]{0:T(128)}, u32[]{:S(2)}) copy-start(f32[8]{0:T(128)} %refs_3_.1) | copy-start | bytes 100
  0.7 0.8 %copy-start = (f32[8,8,128]{2,1,0:T(8,128)S(1)}, f32[8,8,128]{2,1,0:T(8,128)}, u32[]{:S(2)}) copy-start(f32[8,8,128]{2,1,0:T(8,128)} %refs_1_.1) | copy-start | bytes 98308
  1.4 0.7 copy-start.3

commit v5 on v4

--- a/solution.py
+++ b/solution.py
@@ -152,30 +152,40 @@
         wide[pair, 0:16] = block[1008:1024]
         wide[pair, 1040:1056] = block[0:16]
 
-    def block_copy(t, to):
+    parts = [(0, 0, 160), (1, 0, 160), (2, 0, 96), (3, 0, 96), (2, 96, 160), (3, 96, 160)]
+
+    def block_copy(q, to):
+        t, low, high = parts[q]
         return remote(
-            wide.at[pair_of(t, half), pl.ds(pl.multiple_of(128 * to, 128), 160)],
-            rcv.at[place_of(t, half), mem], block_send.at[t, to], block_recv.at[t, slot], ring, to,
+            wide.at[
+                pair_of(t, half), pl.ds(pl.multiple_of(128 * to + low, 16), high - low)
+            ],
+            rcv.at[place_of(t, half), mem, low:high], block_send.at[q, to],
+            block_recv.at[q, slot], ring, to,
         )
 
-    def own_copy(t):
+    def own_copy(q):
+        t, low, high = parts[q]
         return pltpu.make_async_copy(
-            wide.at[pair_of(t, half), pl.ds(pl.multiple_of(128 * slot, 128), 160)],
-            rcv.at[place_of(t, half), mem], block_recv.at[t, slot],
+            wide.at[
+                pair_of(t, half), pl.ds(pl.multiple_of(128 * slot + low, 16), high - low)
+            ],
+            rcv.at[place_of(t, half), mem, low:high], block_recv.at[q, slot],
         )
 
-    def send_blocks(t):
-        loop(1, 8, lambda j: block_copy(t, lax.rem(slot + j, 8)).start())
-        own_copy(t).start()
-
-    def wait_blocks(t):
-        own_copy(t).wait()
+    def send_blocks(q):
+        loop(1, 8, lambda j: block_copy(q, lax.rem(slot + j, 8)).start())
+        own_copy(q).start()
+
+    def wait_blocks(q):
+        own_copy(q).wait()
+        t, low, high = parts[q]
 
         def wait(j):
             frm = lax.rem(slot + j, 8)
             remote(
-                wide.at[0, 0:160], rcv.at[place_of(t, frm // 4), lax.rem(frm, 4)],
-                block_send.at[t, frm], block_recv.at[t, frm], ring, frm,
+                wide.at[0, low:high], rcv.at[place_of(t, frm // 4), lax.rem(frm, 4), low:high],
+                block_send.at[q, frm], block_recv.at[q, frm], ring, frm,
             ).wait_recv()
 
         loop(1, 8, wait)
@@ -239,7 +249,8 @@
 
     turn_pair(3)
     loop(1, 8, lambda j: block_copy(1, lax.rem(slot + j, 8)).wait_send())
-    send_blocks(3)
+    for q in (3, 4, 5):
+        send_blocks(q)
 
     def spread_row(i):
         lane = lax.broadcasted_iota(jnp.int32, (20, 8, 128), 2)
@@ -262,28 +273,30 @@
             speed = jnp.where(sublane == f, ref[f], speed)
         wt_ref[4 + k] = speed
 
-    def unshuffle(pair):
-        low = lax.broadcasted_iota(jnp.int32, (160, 128), 1) < 64
+    def unshuffle(pair, y0=0, y1=20):
+        low = lax.broadcasted_iota(jnp.int32, (8 * (y1 - y0), 128), 1) < 64
+        rows = slice(8 * y0, 8 * y1)
         for mh in range(2):
-            r0 = rcv[pair, 2 * mh].astype(F32)
-            r1 = rcv[pair, 2 * mh + 1].astype(F32)
+            r0 = rcv[pair, 2 * mh, rows].astype(F32)
+            r1 = rcv[pair, 2 * mh + 1, rows].astype(F32)
             even = jnp.where(low, r0, pltpu.roll(r1, 64, 1))
             odd = jnp.where(low, pltpu.roll(r0, 64, 1), r1)
-            u0[mh, 2 * pair] = even.reshape(20, 8, 128)
-            u0[mh, 2 * pair + 1] = odd.reshape(20, 8, 128)
+            u0[mh, 2 * pair, y0:y1] = even.reshape(y1 - y0, 8, 128)
+            u0[mh, 2 * pair + 1, y0:y1] = odd.reshape(y1 - y0, 8, 128)
 
     unshuffle(1)
     unshuffle(8)
     sx = wt_ref[4][None]
     sy = wt_ref[5][None]
 
-    def first(x):
-        s = coef[x, 1:19]
+    def first(x, y0=0, y1=18):
+        s = coef[x, y0 + 1 : y1 + 1]
+        here, behind, ahead = slice(y0 + 1, y1 + 1), slice(y0, y1), slice(y0 + 2, y1 + 2)
         for mh in range(2):
-            u1[mh, x - 1] = rounded(
+            u1[mh, x - 1, y0:y1] = rounded(
                 stencil(
-                    u0[mh, x, 1:19], u0[mh, x - 1, 1:19], u0[mh, x + 1, 1:19],
-                    u0[mh, x, 0:18], u0[mh, x, 2:20], s, sx, sy,
+                    u0[mh, x, here], u0[mh, x - 1, here], u0[mh, x + 1, here],
+                    u0[mh, x, behind], u0[mh, x, ahead], s, sx, sy,
                 )
             )
 
@@ -308,28 +321,24 @@
                 (prior[mh] - centre).reshape(64, 128).astype(BF16)
             )
 
-    def firsts(low, high):
+    def firsts(low, high, y0=0, y1=18):
         def both(k):
-            first(low + k)
-            first(high + k)
+            first(low + k, y0, y1)
+            first(high + k, y0, y1)
 
         loop(0, 2, both)
 
-    def seconds(low, high):
+    def seconds(low, high, c):
         def both(k):
-            for c in range(2):
-                second(low + k, c)
-                second(high + k, c)
+            second(low + k, c)
+            second(high + k, c)
 
         loop(0, 2, both)
 
-    def inwards(t):
-        wait_blocks(t)
-        unshuffle(1 + t)
-        unshuffle(8 - t)
-        firsts(2 * t + 1, 17 - 2 * t)
-
-    loop(1, 3, inwards)
+    wait_blocks(1)
+    unshuffle(2)
+    unshuffle(7)
+    firsts(3, 15)
     for copy in spr_far:
         copy.wait()
     for i in (0, 1, 18, 19):
@@ -339,21 +348,14 @@
     unshuffle(0)
     unshuffle(9)
     firsts(1, 17)
-
-    def outer(t):
-        seconds(2 * t, 14 - 2 * t)
-
-    loop(0, 2, outer)
-
-    def count_wait(j):
-        frm = lax.rem(ring + j, rings)
-        remote(cst.at[0], cra.at[frm], cnt_send.at[j], cnt_recv.at[frm], frm, slot).wait_recv()
-
-    loop(1, rings, count_wait)
-    total = cra[0]
-    for r in range(1, rings):
-        total = total + cra[r]
-    crb[slot] = total
+    for c in range(2):
+        seconds(0, 14, c)
+
+    row = lax.broadcasted_iota(jnp.int32, (128, 128), 0)
+    col = lax.broadcasted_iota(jnp.int32, (128, 128), 1)
+    left = lax.rem(slot + 7, 8)
+    right = lax.rem(slot + 1, 8)
+    copies = []
 
     def sum_copy(j):
         return remote(
@@ -361,22 +363,31 @@
             lax.rem(slot + j, 8),
         )
 
-    loop(1, 8, lambda j: sum_copy(j).start())
-
-    wait_blocks(3)
-    unshuffle(4)
-    unshuffle(5)
-    loop(7, 13, first)
-
-    row = lax.broadcasted_iota(jnp.int32, (128, 128), 0)
-    col = lax.broadcasted_iota(jnp.int32, (128, 128), 1)
-    left = lax.rem(slot + 7, 8)
-    right = lax.rem(slot + 1, 8)
-    copies = []
     for c in range(2):
+        if c:
+            def count_wait(j):
+                frm = lax.rem(ring + j, rings)
+                remote(cst.at[0], cra.at[frm], cnt_send.at[j], cnt_recv.at[frm], frm, slot).wait_recv()
+
+            loop(1, rings, count_wait)
+            total = cra[0]
+            for r in range(1, rings):
+                total = total + cra[r]
+            crb[slot] = total
+
+            loop(1, 8, lambda j: sum_copy(j).start())
+        (y0, y1), (z0, z1) = (((0, 12), (0, 10)), ((12, 20), (10, 18)))[c]
+        wait_blocks(2 + 2 * c)
+        unshuffle(3, y0, y1)
+        unshuffle(6, y0, y1)
+        firsts(5, 13, z0, z1)
+        seconds(2, 12, c)
+        wait_blocks(3 + 2 * c)
+        unshuffle(4, y0, y1)
+        unshuffle(5, y0, y1)
+        loop(7, 13, lambda x, z0=z0, z1=z1: first(x, z0, z1))
         for h in range(2):
             p = 2 * h + c
-
             loop(4 + 4 * h, 8 + 4 * h, lambda row, c=c: second(row, c))
             a = anom_ref[p].reshape(512, 256)
             g = lax.dot_general(a, a, TN, preferred_element_type=F32) * (1.0 / 512.0)
@@ -417,8 +428,8 @@
             wt_ref[2 * h + c] = jnp.broadcast_to(count / (count + 16.0), (8, 128))
     loop(1, rings, lambda j: count_copy(j).wait_send())
     loop(1, 8, lambda j: sum_copy(j).wait_send())
-    for t in (0, 2, 3):
-        loop(1, 8, lambda j, t=t: block_copy(t, lax.rem(slot + j, 8)).wait_send())
+    for q in (0, 2, 3, 4, 5):
+        loop(1, 8, lambda j, q=q: block_copy(q, lax.rem(slot + j, 8)).wait_send())
     for copy in copies:
         copy.wait()
     for c in range(2):
@@ -736,8 +747,8 @@
             pltpu.VMEM((2, 264, 128), F32),
             pltpu.VMEM((2, 264, 128), F32),
             DMA((3,)),
-            DMA((4, 8)),
-            DMA((4, 8)),
+            DMA((6, 8)),
+            DMA((6, 8)),
             DMA((2,)),
             DMA((2,)),
             DMA((3,)),

time: 67.3 us -> 65.8 us (0.978)
  Pallas kernels: 62.5 us -> 61 us
    pallas_call x1, Pallas kernels: 20 us -> 19 us  [local(): pl.pallas_call(lambda *refs: return_kernel(rings, *refs), out_shape=shape...]
where the time goes in v5:
time: 65.8 us; the launch traced here: 65.6 us
  Pallas kernels  61 us (93%)
  local copies, waits for them, and re-layouts  4.55 us (7%)
    pallas_call x1, Pallas kernels, local(): pl.pallas_call(lambda *refs: forecast_kernel(rings, *refs), out_shape=[sh...  39 us
    pallas_call x1, Pallas kernels, local(): pl.pallas_call(lambda *refs: return_kernel(rings, *refs), out_shape=shape...  19 us
    pallas_call x1, Pallas kernels, local(): pl.pallas_call(analysis_kernel, out_shape=[square, square, square, square...  2.94 us
    unnamed x9, local copies, waits for them, and re-layouts  2.36 us
    reshape x1, local copies, waits for them, and re-layouts, local(): return jnp.transpose(out.reshape(8, 64, 8, 128), (1, 2, 0, 3))  2.2 us

profile of v5, /device:TPU:1, one launch (start us, length us, event | category | flops | bytes accessed | tf_op | source)
XLA Modules:
  0.0 65.6 jit_solution(15895752695125989183)
XLA Ops:
  0.0 0.0 copy-start.1
  0.0 0.0 copy-start.2
  0.0 0.7 %copy-done.1 = s32[256]{0:T(256)S(1)} copy-done((s32[256]{0:T(256)S(1)}, s32[256]{0:T(256)}, u32[]{:S(2)}) %copy-start.1) | copy-done | bytes 1048
  0.7 0.0 copy-done.2
  0.7 0.0 copy-start
  0.7 0.8 %copy-done = f32[8,8,128]{2,1,0:T(8,128)S(1)} copy-done((f32[8,8,128]{2,1,0:T(8,128)S(1)}, f32[8,8,128]{2,1,0:T(8,128)}, u32[]{:S(2)}) %copy-start) | copy-done | bytes 32792
  1.4 0.0 copy-start.3
  1.4 0.7 copy-done.3
  2.1 39.0 %shard_map.55 = (bf16[4,8,64,256]{3,2,1,0:T(8,128)(2,1)S(1)}, f32[4,8,64,128]{3,2,1,0:T(8,128)S(1)}, f32[4,264,128]{2,1,0:T(8,128)S(1)}, f32[6,8,128]{2,1,0:T(8,128)S(1)}, f32[16,16,8,128]{3,2,1,0:T(8,128)S(1)}) custom-call(bf16[64,8,8,128]{3,2,1,0:T(8,128)(2,1)} %refs_0_.1, f32[8,8,128]{2,1,0:T(8,128)S(1)} %copy-done, s32[1,256]{1,0:T(1,128)S(1)} %bitcast.9, ...), custom_call_target="tpu_custom_call" | custom-call | tf_op jit(solution)/shard_map/pallas_call | solution.py:716
  41.1 2.9 %shard_map.56 = (bf16[4,256,256]{2,1,0:T(8,128)(2,1)S(1)}, bf16[4,256,256]{2,1,0:T(8,128)(2,1)S(1)}, bf16[4,256,256]{2,1,0:T(8,128)(2,1)S(1)}, bf16[4,256,256]{2,1,0:T(8,128)(2,1)S(1)}, f32[12,8,128]{2,1,0:T(8,128)S(1)}) custom-call(f32[4,264,128]{2,1,0:T(8,128)S(1)} %get-tuple-element.17.avg_ref, f32[6,8,128]{2,1,0:T(8,128)S(1)} %get-tuple-element.18.wt_ref.refs_8_), custom_call_target="tpu_custom_call" | custom-call | tf_op jit(solution)/shard_map/pallas_call | solution.py:769
  44.1 19.0 %shard_map.57 = bf16[8,64,1024]{2,1,0:T(8,128)(2,1)S(1)} custom-call(bf16[4,8,64,256]{3,2,1,0:T(8,128)(2,1)S(1)} %get-tuple-element.15.refs_0_, f32[4,8,64,128]{3,2,1,0:T(8,128)S(1)} %get-tuple-element.16.refs_1_, bf16[4,256,256]{2,1,0:T(8,128)(2,1)S(1)} %get-tuple-element.19.refs_2_, bf16[4,256,256]{2,1,0:T(8,128)(2,1)S(1)} %get-tuple-element.20.refs_3_, ...), custom_call_target="tpu_custom_call" | custom-call | tf_op jit(solution)/shard_map/pallas_call | solution.py:778
  63.1 0.3 copy.7
  63.4 2.2 %copy.9 = bf16[8,64,8,128]{3,0,2,1:T(8,128)(2,1)} copy(bf16[8,64,8,128]{3,2,1,0:T(8,128)(2,1)S(1)} %bitcast.10) | data formatting | bytes 2097152 | tf_op jit(solution)/shard_map/reshape | solution.py:802
Async XLA Ops:
  0.0 0.7 %copy-start.1 = (s32[256]{0:T(256)S(1)}, s32[256]{0:T(256)}, u32[]{:S(2)}) copy-start(s32[256]{0:T(256)} %param.9) | copy-start | bytes 3076
  0.0 0.7 %copy-start.2 = (f32[8]{0:T(128)S(1)}, f32[8]{0:T(128)}, u32[]{:S(2)}) copy-start(f32[8]{0:T(128)} %refs_3_.1) | copy-start | bytes 100
  0.7 0.8 %copy-start = (f32[8,8,128]{2,1,0:T(8,128)S(1)}, f32[8,8,128]{2,1,0:T(8,128)}, u32[]{:S(2)}) copy-start(f32[8,8,128]{2,1,0:T(8,128)} %refs_1_.1) | copy-start | bytes 98308
  1.4 0.7 copy-start.3

commit v6 on v5

--- a/solution.py
+++ b/solution.py
@@ -645,7 +645,8 @@
 
     for h in range(2):
         loop(1 - h, 4 - h, lambda pair, h=h: step_pair(h, pair, 2, 14))
-    send(0)
+        skip = half if h else 1 - half
+        loop(skip, 4, lambda j, h=h: main_copy(0, 4 * h + lax.rem(mem + j, 4)).start())
     for copy in edges:
         copy.wait()
     for mh in range(2):

time: 65.8 us -> 65.5 us (level)
  no operation moved by 1% of the time
where the time goes in v6:
time: 65.5 us; the launch traced here: 65.3 us
  Pallas kernels  60.7 us (93%)
  local copies, waits for them, and re-layouts  4.55 us (7%)
    pallas_call x1, Pallas kernels, local(): pl.pallas_call(lambda *refs: forecast_kernel(rings, *refs), out_shape=[sh...  39 us
    pallas_call x1, Pallas kernels, local(): pl.pallas_call(lambda *refs: return_kernel(rings, *refs), out_shape=shape...  18.7 us
    pallas_call x1, Pallas kernels, local(): pl.pallas_call(analysis_kernel, out_shape=[square, square, square, square...  2.94 us
    unnamed x9, local copies, waits for them, and re-layouts  2.36 us
    reshape x1, local copies, waits for them, and re-layouts, local(): return jnp.transpose(out.reshape(8, 64, 8, 128), (1, 2, 0, 3))  2.2 us

profile of v6, /device:TPU:1, one launch (start us, length us, event | category | flops | bytes accessed | tf_op | source)
XLA Modules:
  0.0 65.3 jit_solution(11717153000997927823)
XLA Ops:
  0.0 0.0 copy-start.1
  0.0 0.0 copy-start.2
  0.0 0.7 %copy-done.1 = s32[256]{0:T(256)S(1)} copy-done((s32[256]{0:T(256)S(1)}, s32[256]{0:T(256)}, u32[]{:S(2)}) %copy-start.1) | copy-done | bytes 1048
  0.7 0.0 copy-done.2
  0.7 0.0 copy-start
  0.7 0.8 %copy-done = f32[8,8,128]{2,1,0:T(8,128)S(1)} copy-done((f32[8,8,128]{2,1,0:T(8,128)S(1)}, f32[8,8,128]{2,1,0:T(8,128)}, u32[]{:S(2)}) %copy-start) | copy-done | bytes 32792
  1.4 0.0 copy-start.3
  1.4 0.7 %copy-done.3 = f32[8]{0:T(128)S(1)} copy-done((f32[8]{0:T(128)S(1)}, f32[8]{0:T(128)}, u32[]{:S(2)}) %copy-start.3) | copy-done | bytes 56
  2.1 39.0 %shard_map.55 = (bf16[4,8,64,256]{3,2,1,0:T(8,128)(2,1)S(1)}, f32[4,8,64,128]{3,2,1,0:T(8,128)S(1)}, f32[4,264,128]{2,1,0:T(8,128)S(1)}, f32[6,8,128]{2,1,0:T(8,128)S(1)}, f32[16,16,8,128]{3,2,1,0:T(8,128)S(1)}) custom-call(bf16[64,8,8,128]{3,2,1,0:T(8,128)(2,1)} %refs_0_.1, f32[8,8,128]{2,1,0:T(8,128)S(1)} %copy-done, s32[1,256]{1,0:T(1,128)S(1)} %bitcast.9, ...), custom_call_target="tpu_custom_call" | custom-call | tf_op jit(solution)/shard_map/pallas_call | solution.py:717
  41.1 2.9 %shard_map.56 = (bf16[4,256,256]{2,1,0:T(8,128)(2,1)S(1)}, bf16[4,256,256]{2,1,0:T(8,128)(2,1)S(1)}, bf16[4,256,256]{2,1,0:T(8,128)(2,1)S(1)}, bf16[4,256,256]{2,1,0:T(8,128)(2,1)S(1)}, f32[12,8,128]{2,1,0:T(8,128)S(1)}) custom-call(f32[4,264,128]{2,1,0:T(8,128)S(1)} %get-tuple-element.17.avg_ref, f32[6,8,128]{2,1,0:T(8,128)S(1)} %get-tuple-element.18.wt_ref.refs_8_), custom_call_target="tpu_custom_call" | custom-call | tf_op jit(solution)/shard_map/pallas_call | solution.py:770
  44.1 18.7 %shard_map.57 = bf16[8,64,1024]{2,1,0:T(8,128)(2,1)S(1)} custom-call(bf16[4,8,64,256]{3,2,1,0:T(8,128)(2,1)S(1)} %get-tuple-element.15.refs_0_, f32[4,8,64,128]{3,2,1,0:T(8,128)S(1)} %get-tuple-element.16.refs_1_, bf16[4,256,256]{2,1,0:T(8,128)(2,1)S(1)} %get-tuple-element.19.refs_2_, bf16[4,256,256]{2,1,0:T(8,128)(2,1)S(1)} %get-tuple-element.20.refs_3_, ...), custom_call_target="tpu_custom_call" | custom-call | tf_op jit(solution)/shard_map/pallas_call | solution.py:779
  62.8 0.3 copy.7
  63.1 2.2 %copy.9 = bf16[8,64,8,128]{3,0,2,1:T(8,128)(2,1)} copy(bf16[8,64,8,128]{3,2,1,0:T(8,128)(2,1)S(1)} %bitcast.10) | data formatting | bytes 2097152 | tf_op jit(solution)/shard_map/reshape | solution.py:803
Async XLA Ops:
  0.0 0.7 %copy-start.1 = (s32[256]{0:T(256)S(1)}, s32[256]{0:T(256)}, u32[]{:S(2)}) copy-start(s32[256]{0:T(256)} %param.9) | copy-start | bytes 3076
  0.0 0.7 %copy-start.2 = (f32[8]{0:T(128)S(1)}, f32[8]{0:T(128)}, u32[]{:S(2)}) copy-start(f32[8]{0:T(128)} %refs_3_.1) | copy-start | bytes 100
  0.7 0.8 %copy-start = (f32[8,8,128]{2,1,0:T(8,128)S(1)}, f32[8,8,128]{2,1,0:T(8,128)}, u32[]{:S(2)}) copy-start(f32[8,8,128]{2,1,0:T(8,128)} %refs_1_.1) | copy-start | bytes 98308
  1.4 0.7 %copy-start.3 = (f32[8]{0:T(128)S(1)}, f32[8]{0:T(128)}, u32[]{:S(2)}) copy-start(f32[8]{0:T(128)} %refs_4_.1) | copy-start | bytes 100

commit v7 on v6

--- a/solution.py
+++ b/solution.py
@@ -248,10 +248,6 @@
         copy.start()
 
     turn_pair(3)
-    loop(1, 8, lambda j: block_copy(1, lax.rem(slot + j, 8)).wait_send())
-    for q in (3, 4, 5):
-        send_blocks(q)
-
     def spread_row(i):
         lane = lax.broadcasted_iota(jnp.int32, (20, 8, 128), 2)
         column = lax.rem(
@@ -272,6 +268,10 @@
         for f in range(8):
             speed = jnp.where(sublane == f, ref[f], speed)
         wt_ref[4 + k] = speed
+
+    loop(1, 8, lambda j: block_copy(1, lax.rem(slot + j, 8)).wait_send())
+    for q in (3, 4, 5):
+        send_blocks(q)
 
     def unshuffle(pair, y0=0, y1=20):
         low = lax.broadcasted_iota(jnp.int32, (8 * (y1 - y0), 128), 1) < 64

time: 65.5 us -> 66.9 us (1.021)
  Pallas kernels: 60.7 us -> 62 us
    pallas_call x1, Pallas kernels: 2.94 us -> 4.44 us  [local(): pl.pallas_call(analysis_kernel, out_shape=[square, square, square, square...]
where the time goes in v7:
time: 66.9 us; the launch traced here: 66.6 us
  Pallas kernels  62 us (93%)
  local copies, waits for them, and re-layouts  4.55 us (7%)
    pallas_call x1, Pallas kernels, local(): pl.pallas_call(lambda *refs: forecast_kernel(rings, *refs), out_shape=[sh...  39 us
    pallas_call x1, Pallas kernels, local(): pl.pallas_call(lambda *refs: return_kernel(rings, *refs), out_shape=shape...  18.6 us
    pallas_call x1, Pallas kernels, local(): pl.pallas_call(analysis_kernel, out_shape=[square, square, square, square...  4.44 us
    unnamed x9, local copies, waits for them, and re-layouts  2.36 us
    reshape x1, local copies, waits for them, and re-layouts, local(): return jnp.transpose(out.reshape(8, 64, 8, 128), (1, 2, 0, 3))  2.2 us

profile of v7, /device:TPU:1, one launch (start us, length us, event | category | flops | bytes accessed | tf_op | source)
XLA Modules:
  0.0 66.6 jit_solution(13233857723918762280)
XLA Ops:
  0.0 0.0 copy-start.1
  0.0 0.0 copy-start.2
  0.0 0.7 %copy-done.1 = s32[256]{0:T(256)S(1)} copy-done((s32[256]{0:T(256)S(1)}, s32[256]{0:T(256)}, u32[]{:S(2)}) %copy-start.1) | copy-done | bytes 1048
  0.7 0.0 copy-done.2
  0.7 0.0 copy-start
  0.7 0.8 %copy-done = f32[8,8,128]{2,1,0:T(8,128)S(1)} copy-done((f32[8,8,128]{2,1,0:T(8,128)S(1)}, f32[8,8,128]{2,1,0:T(8,128)}, u32[]{:S(2)}) %copy-start) | copy-done | bytes 32792
  1.4 0.0 copy-start.3
  1.4 0.7 copy-done.3
  2.1 39.0 %shard_map.55 = (bf16[4,8,64,256]{3,2,1,0:T(8,128)(2,1)S(1)}, f32[4,8,64,128]{3,2,1,0:T(8,128)S(1)}, f32[4,264,128]{2,1,0:T(8,128)S(1)}, f32[6,8,128]{2,1,0:T(8,128)S(1)}, f32[16,16,8,128]{3,2,1,0:T(8,128)S(1)}) custom-call(bf16[64,8,8,128]{3,2,1,0:T(8,128)(2,1)} %refs_0_.1, f32[8,8,128]{2,1,0:T(8,128)S(1)} %copy-done, s32[1,256]{1,0:T(1,128)S(1)} %bitcast.9, ...), custom_call_target="tpu_custom_call" | custom-call | tf_op jit(solution)/shard_map/pallas_call | solution.py:717
  41.1 4.4 %shard_map.56 = (bf16[4,256,256]{2,1,0:T(8,128)(2,1)S(1)}, bf16[4,256,256]{2,1,0:T(8,128)(2,1)S(1)}, bf16[4,256,256]{2,1,0:T(8,128)(2,1)S(1)}, bf16[4,256,256]{2,1,0:T(8,128)(2,1)S(1)}, f32[12,8,128]{2,1,0:T(8,128)S(1)}) custom-call(f32[4,264,128]{2,1,0:T(8,128)S(1)} %get-tuple-element.17.avg_ref, f32[6,8,128]{2,1,0:T(8,128)S(1)} %get-tuple-element.18.wt_ref.refs_8_), custom_call_target="tpu_custom_call" | custom-call | tf_op jit(solution)/shard_map/pallas_call | solution.py:770
  45.6 18.6 %shard_map.57 = bf16[8,64,1024]{2,1,0:T(8,128)(2,1)S(1)} custom-call(bf16[4,8,64,256]{3,2,1,0:T(8,128)(2,1)S(1)} %get-tuple-element.15.refs_0_, f32[4,8,64,128]{3,2,1,0:T(8,128)S(1)} %get-tuple-element.16.refs_1_, bf16[4,256,256]{2,1,0:T(8,128)(2,1)S(1)} %get-tuple-element.19.refs_2_, bf16[4,256,256]{2,1,0:T(8,128)(2,1)S(1)} %get-tuple-element.20.refs_3_, ...), custom_call_target="tpu_custom_call" | custom-call | tf_op jit(solution)/shard_map/pallas_call | solution.py:779
  64.2 0.3 copy.7
  64.4 2.2 %copy.9 = bf16[8,64,8,128]{3,0,2,1:T(8,128)(2,1)} copy(bf16[8,64,8,128]{3,2,1,0:T(8,128)(2,1)S(1)} %bitcast.10) | data formatting | bytes 2097152 | tf_op jit(solution)/shard_map/reshape | solution.py:803
Async XLA Ops:
  0.0 0.7 %copy-start.1 = (s32[256]{0:T(256)S(1)}, s32[256]{0:T(256)}, u32[]{:S(2)}) copy-start(s32[256]{0:T(256)} %param.9) | copy-start | bytes 3076
  0.0 0.7 %copy-start.2 = (f32[8]{0:T(128)S(1)}, f32[8]{0:T(128)}, u32[]{:S(2)}) copy-start(f32[8]{0:T(128)} %refs_3_.1) | copy-start | bytes 100
  0.7 0.8 %copy-start = (f32[8,8,128]{2,1,0:T(8,128)S(1)}, f32[8,8,128]{2,1,0:T(8,128)}, u32[]{:S(2)}) copy-start(f32[8,8,128]{2,1,0:T(8,128)} %refs_1_.1) | copy-start | bytes 98308
  1.4 0.7 copy-start.3

commit v8 on v7

--- a/solution.py
+++ b/solution.py
@@ -207,6 +207,7 @@
     turn_pair(1)
     send_blocks(1)
     turn_pair(2)
+    turn_pair(3)
 
     load_obs.wait()
     obs = obs_in[...]
@@ -247,7 +248,6 @@
     for copy in spr_far:
         copy.start()
 
-    turn_pair(3)
     def spread_row(i):
         lane = lax.broadcasted_iota(jnp.int32, (20, 8, 128), 2)
         column = lax.rem(

time: 66.9 us -> 65.4 us (0.978)
  Pallas kernels: 62 us -> 60.7 us
    pallas_call x1, Pallas kernels: 4.44 us -> 2.94 us  [local(): pl.pallas_call(analysis_kernel, out_shape=[square, square, square, square...]
where the time goes in v8:
time: 65.4 us; the launch traced here: 65.3 us
  Pallas kernels  60.7 us (93%)
  local copies, waits for them, and re-layouts  4.55 us (7%)
    pallas_call x1, Pallas kernels, local(): pl.pallas_call(lambda *refs: forecast_kernel(rings, *refs), out_shape=[sh...  39 us
    pallas_call x1, Pallas kernels, local(): pl.pallas_call(lambda *refs: return_kernel(rings, *refs), out_shape=shape...  18.8 us
    pallas_call x1, Pallas kernels, local(): pl.pallas_call(analysis_kernel, out_shape=[square, square, square, square...  2.94 us
    unnamed x9, local copies, waits for them, and re-layouts  2.36 us
    reshape x1, local copies, waits for them, and re-layouts, local(): return jnp.transpose(out.reshape(8, 64, 8, 128), (1, 2, 0, 3))  2.2 us

profile of v8, /device:TPU:1, one launch (start us, length us, event | category | flops | bytes accessed | tf_op | source)
XLA Modules:
  0.0 65.3 jit_solution(5608715001723665042)
XLA Ops:
  0.0 0.0 copy-start.1
  0.0 0.0 copy-start.2
  0.0 0.7 %copy-done.1 = s32[256]{0:T(256)S(1)} copy-done((s32[256]{0:T(256)S(1)}, s32[256]{0:T(256)}, u32[]{:S(2)}) %copy-start.1) | copy-done | bytes 1048
  0.7 0.0 copy-done.2
  0.7 0.0 copy-start
  0.7 0.8 %copy-done = f32[8,8,128]{2,1,0:T(8,128)S(1)} copy-done((f32[8,8,128]{2,1,0:T(8,128)S(1)}, f32[8,8,128]{2,1,0:T(8,128)}, u32[]{:S(2)}) %copy-start) | copy-done | bytes 32792
  1.4 0.0 copy-start.3
  1.4 0.7 copy-done.3
  2.1 39.0 %shard_map.55 = (bf16[4,8,64,256]{3,2,1,0:T(8,128)(2,1)S(1)}, f32[4,8,64,128]{3,2,1,0:T(8,128)S(1)}, f32[4,264,128]{2,1,0:T(8,128)S(1)}, f32[6,8,128]{2,1,0:T(8,128)S(1)}, f32[16,16,8,128]{3,2,1,0:T(8,128)S(1)}) custom-call(bf16[64,8,8,128]{3,2,1,0:T(8,128)(2,1)} %refs_0_.1, f32[8,8,128]{2,1,0:T(8,128)S(1)} %copy-done, s32[1,256]{1,0:T(1,128)S(1)} %bitcast.9, ...), custom_call_target="tpu_custom_call" | custom-call | tf_op jit(solution)/shard_map/pallas_call | solution.py:717
  41.1 2.9 %shard_map.56 = (bf16[4,256,256]{2,1,0:T(8,128)(2,1)S(1)}, bf16[4,256,256]{2,1,0:T(8,128)(2,1)S(1)}, bf16[4,256,256]{2,1,0:T(8,128)(2,1)S(1)}, bf16[4,256,256]{2,1,0:T(8,128)(2,1)S(1)}, f32[12,8,128]{2,1,0:T(8,128)S(1)}) custom-call(f32[4,264,128]{2,1,0:T(8,128)S(1)} %get-tuple-element.17.avg_ref, f32[6,8,128]{2,1,0:T(8,128)S(1)} %get-tuple-element.18.wt_ref.refs_8_), custom_call_target="tpu_custom_call" | custom-call | tf_op jit(solution)/shard_map/pallas_call | solution.py:770
  44.1 18.8 %shard_map.57 = bf16[8,64,1024]{2,1,0:T(8,128)(2,1)S(1)} custom-call(bf16[4,8,64,256]{3,2,1,0:T(8,128)(2,1)S(1)} %get-tuple-element.15.refs_0_, f32[4,8,64,128]{3,2,1,0:T(8,128)S(1)} %get-tuple-element.16.refs_1_, bf16[4,256,256]{2,1,0:T(8,128)(2,1)S(1)} %get-tuple-element.19.refs_2_, bf16[4,256,256]{2,1,0:T(8,128)(2,1)S(1)} %get-tuple-element.20.refs_3_, ...), custom_call_target="tpu_custom_call" | custom-call | tf_op jit(solution)/shard_map/pallas_call | solution.py:779
  62.8 0.3 copy.7
  63.1 2.2 %copy.9 = bf16[8,64,8,128]{3,0,2,1:T(8,128)(2,1)} copy(bf16[8,64,8,128]{3,2,1,0:T(8,128)(2,1)S(1)} %bitcast.10) | data formatting | bytes 2097152 | tf_op jit(solution)/shard_map/reshape | solution.py:803
Async XLA Ops:
  0.0 0.7 %copy-start.1 = (s32[256]{0:T(256)S(1)}, s32[256]{0:T(256)}, u32[]{:S(2)}) copy-start(s32[256]{0:T(256)} %param.9) | copy-start | bytes 3076
  0.0 0.7 %copy-start.2 = (f32[8]{0:T(128)S(1)}, f32[8]{0:T(128)}, u32[]{:S(2)}) copy-start(f32[8]{0:T(128)} %refs_3_.1) | copy-start | bytes 100
  0.7 0.8 %copy-start = (f32[8,8,128]{2,1,0:T(8,128)S(1)}, f32[8,8,128]{2,1,0:T(8,128)}, u32[]{:S(2)}) copy-start(f32[8,8,128]{2,1,0:T(8,128)} %refs_1_.1) | copy-start | bytes 98308
  1.4 0.7 %copy-start.3 = (f32[8]{0:T(128)S(1)}, f32[8]{0:T(128)}, u32[]{:S(2)}) copy-start(f32[8]{0:T(128)} %refs_4_.1) | copy-start | bytes 100
